TPU v7x, 32 devices: a whole 2x2x4 slice. The times are simulated.
32 devices in a mesh: dp: 8 (over z, x), tensor: 4 (over y, core).
Axes of the slice: x: 2, y: 2, z: 4, core: 2. Of those that a mesh axis runs over, the one named last changes fastest.
Arguments:
- layer_input: bfloat16 [4096, 768], P('dp', 'tensor'), may hold values from -6 to 6
- segment_ids: int32 [8, 512], P('dp'), may hold values from 0 to 15, never falling along the last dimension, each value on 1 to 256 neighbouring positions
- triple_weight: bfloat16 [768, 3, 768], P(None, None, 'tensor'), may hold values from -0.21875 to 0.21875
- query_value_bias: float32 [2, 768], P(None, 'tensor'), may hold values from -3 to 3
- output_weight: bfloat16 [768, 768], P('tensor'), may hold values from -0.875 to 0.875
- output_bias: float32 [768], P('tensor'), may hold values from -3 to 3
- norm_gain: float32 [768], P('tensor'), may hold values from 0.5 to 1.5
- norm_shift: float32 [768], P('tensor'), may hold values from -3 to 3
- expand_weight: bfloat16 [768, 3072], P(None, 'tensor'), may hold values from -0.21875 to 0.21875
- expand_bias: float32 [3072], P('tensor'), may hold values from -3 to 3
- reduce_weight: bfloat16 [3072, 768], P('tensor'), may hold values from -0.109375 to 0.109375
- reduce_bias: float32 [768], P('tensor'), may hold values from -3 to 3
- final_gain: float32 [768], P('tensor'), may hold values from 0.5 to 1.5
- final_shift: float32 [768], P('tensor'), may hold values from -3 to 3
- cotangent: bfloat16 [4096, 768], P('dp', 'tensor'), may hold values from -6 to 6
Outputs:
- layer_output: bfloat16 [4096, 768], P('dp', 'tensor')
- input_grad: float32 [4096, 768], P('dp', 'tensor')
- triple_grad: float32 [768, 3, 768], P(None, None, 'tensor')
- query_value_grad: float32 [2, 768], P(None, 'tensor')
- output_weight_grad: float32 [768, 768], P('tensor')
- output_bias_grad: float32 [768], P('tensor')
- norm_gain_grad: float32 [768], P('tensor')
- norm_shift_grad: float32 [768], P('tensor')
- expand_weight_grad: float32 [768, 3072], P(None, 'tensor')
- expand_bias_grad: float32 [3072], P('tensor')
- reduce_weight_grad: float32 [3072, 768], P('tensor')
- reduce_bias_grad: float32 [768], P('tensor')
- final_gain_grad: float32 [768], P('tensor')
- final_shift_grad: float32 [768], P('tensor')
Inputs may be any that keep to these rules, and one draw needn't show every extreme that they name: `segment_ids`: segment numbers never fall along a sequence; each document holds 1 to 256 tokens.
All inputs are finite; a program needn't handle non-finite values.
Results may differ from a plain program's by a relative error of at most 0.012.
The roundings to bfloat16 on the way count: a program that leaves them out, or rounds other values in their place, can miss the bound.
Values may be sent and summed in bfloat16 or wider, within the bound.
A program may use at most 64 MiB of HBM per device.

v0:
```python
import jax
import jax.numpy as jnp
from jax import lax
from jax.sharding import PartitionSpec as P

D = 768
HD = 64


EPS = 1e-06


def gelu_value(pre_act):
    return 0.5 * pre_act * (1.0 + lax.erf(pre_act * 0.7071067811865476))


def gelu_slope(pre_act):
    return (
        0.5 * (1.0 + lax.erf(pre_act * 0.7071067811865476))
        + pre_act * jnp.exp(-0.5 * pre_act * pre_act) * 0.3989422804014327
    )


def widen(piece):
    return lax.all_gather(piece, "tensor", axis=1, tiled=True)


def row_stats(first, second):
    return lax.psum((jnp.sum(first, axis=1), jnp.sum(second, axis=1)), "tensor")


def norm_forward(hidden, gain, shift):
    total, squares = row_stats(hidden, hidden * hidden)
    row_mean = (total / D)[:, None]
    inverse = lax.rsqrt(squares[:, None] / D - row_mean * row_mean + EPS)
    normed = (hidden - row_mean) * inverse
    return (normed * gain + shift, normed, inverse)


def norm_backward(upstream, normed, inverse, gain):
    scaled = upstream * gain
    first_total, second_total = row_stats(scaled, scaled * normed)
    return inverse * (scaled - first_total[:, None] / D - normed * second_total[:, None] / D)


def tall_dot(left, right):
    return lax.dot_general(
        left, right, (((0,), (0,)), ((), ())), preferred_element_type=jnp.float32
    )


def wide_dot(left, right):
    return lax.dot_general(
        left, right, (((1,), (1,)), ((), ())), preferred_element_type=jnp.float32
    )


def masked_scores(query_part, key_part, segment_row, head_scale):
    scores = (
        jnp.einsum("qhd,khd->hqk", query_part, key_part, preferred_element_type=jnp.float32)
        * head_scale
    )
    allowed = segment_row[:, None] == segment_row[None, :]
    return jnp.where(allowed[None], scores, -jnp.inf)


def per_device(
    layer_input,
    segment_ids,
    triple_weight,
    query_value_bias,
    output_weight,
    output_bias,
    norm_gain,
    norm_shift,
    expand_weight,
    expand_bias,
    reduce_weight,
    reduce_bias,
    final_gain,
    final_shift,
    cotangent,
):
    seq_count = segment_ids.shape[0]
    seq_len = segment_ids.shape[1]
    tok_count = seq_count * seq_len
    local_width = triple_weight.shape[2]
    local_heads = local_width // HD
    head_scale = HD ** (-0.5)
    gathered = widen(layer_input)
    projected = jnp.einsum(
        "td,dcf->tcf", gathered, triple_weight, preferred_element_type=jnp.float32
    )
    query_half = (
        (projected[:, 0] + query_value_bias[0])
        .astype(jnp.bfloat16)
        .reshape(seq_count, seq_len, local_heads, HD)
    )
    key_half = projected[:, 1].astype(jnp.bfloat16).reshape(seq_count, seq_len, local_heads, HD)
    value_half = (
        (projected[:, 2] + query_value_bias[1])
        .astype(jnp.bfloat16)
        .reshape(seq_count, seq_len, local_heads, HD)
    )
    seq_index = 0
    scores = masked_scores(
        query_half[seq_index], key_half[seq_index], segment_ids[seq_index], head_scale
    )
    top = jnp.max(scores, axis=-1, keepdims=True)
    log_total = top + jnp.log(jnp.sum(jnp.exp(scores - top), axis=-1, keepdims=True))
    probs_half = jnp.exp(scores - log_total).astype(jnp.bfloat16)
    context_list = [
        jnp.einsum(
            "hqk,khd->qhd", probs_half, value_half[seq_index], preferred_element_type=jnp.float32
        ).astype(jnp.bfloat16)
    ]
    total_list = [log_total]
    context = jnp.stack(context_list)
    context_flat = context.reshape(tok_count, local_width)
    attn_share = lax.psum_scatter(
        jnp.dot(context_flat, output_weight, preferred_element_type=jnp.float32),
        "tensor",
        scatter_dimension=1,
        tiled=True,
    )
    first_sum = layer_input.astype(jnp.float32) + attn_share + output_bias
    attended, normed_one, inv_one = norm_forward(first_sum, norm_gain, norm_shift)
    attended_half = widen(attended.astype(jnp.bfloat16))
    pre_act = (
        jnp.dot(attended_half, expand_weight, preferred_element_type=jnp.float32) + expand_bias
    )
    activated = gelu_value(pre_act).astype(jnp.bfloat16)
    mlp_share = lax.psum_scatter(
        jnp.dot(activated, reduce_weight, preferred_element_type=jnp.float32),
        "tensor",
        scatter_dimension=1,
        tiled=True,
    )
    second_sum = attended + mlp_share + reduce_bias
    out_f, normed_two, inv_two = norm_forward(second_sum, final_gain, final_shift)
    layer_output = out_f.astype(jnp.bfloat16)
    upstream = cotangent.astype(jnp.float32)
    final_gain_grad = jnp.sum(upstream * normed_two, axis=0)
    final_shift_grad = jnp.sum(upstream, axis=0)
    second_grad = norm_backward(upstream, normed_two, inv_two, final_gain)
    second_half = widen(second_grad.astype(jnp.bfloat16))
    reduce_weight_grad = tall_dot(activated, second_half)
    reduce_bias_grad = jnp.sum(second_grad, axis=0)
    act_grad = wide_dot(second_half, reduce_weight) * gelu_slope(pre_act)
    act_half = act_grad.astype(jnp.bfloat16)
    expand_weight_grad = tall_dot(attended_half, act_half)
    expand_bias_grad = jnp.sum(act_grad, axis=0)
    attended_grad = second_grad + lax.psum_scatter(
        wide_dot(act_half, expand_weight), "tensor", scatter_dimension=1, tiled=True
    )
    norm_gain_grad = jnp.sum(attended_grad * normed_one, axis=0)
    norm_shift_grad = jnp.sum(attended_grad, axis=0)
    first_grad = norm_backward(attended_grad, normed_one, inv_one, norm_gain)
    first_half = widen(first_grad.astype(jnp.bfloat16))
    output_weight_grad = tall_dot(context_flat, first_half)
    output_bias_grad = jnp.sum(first_grad, axis=0)
    context_grad = (
        wide_dot(first_half, output_weight)
        .astype(jnp.bfloat16)
        .reshape(seq_count, seq_len, local_heads, HD)
    )
    seq_index = 0
    scores = masked_scores(
        query_half[seq_index], key_half[seq_index], segment_ids[seq_index], head_scale
    )
    probs = jnp.exp(scores - total_list[seq_index])
    probs_half = probs.astype(jnp.bfloat16)
    grad_part = context_grad[seq_index]
    value_list = [
        jnp.einsum("hqk,qhd->khd", probs_half, grad_part, preferred_element_type=jnp.float32)
    ]
    prob_grad = jnp.einsum(
        "qhd,khd->hqk", grad_part, value_half[seq_index], preferred_element_type=jnp.float32
    )
    delta = jnp.einsum(
        "qhd,qhd->hq", grad_part.astype(jnp.float32), context[seq_index].astype(jnp.float32)
    )
    score_grad = (probs * (prob_grad - delta[:, :, None]) * head_scale).astype(jnp.bfloat16)
    query_list = [
        jnp.einsum(
            "hqk,khd->qhd", score_grad, key_half[seq_index], preferred_element_type=jnp.float32
        )
    ]
    key_list = [
        jnp.einsum(
            "hqk,qhd->khd", score_grad, query_half[seq_index], preferred_element_type=jnp.float32
        )
    ]
    query_grad = jnp.stack(query_list).reshape(tok_count, local_width)
    key_grad = jnp.stack(key_list).reshape(tok_count, local_width)
    value_grad = jnp.stack(value_list).reshape(tok_count, local_width)
    query_value_grad = jnp.stack([jnp.sum(query_grad, axis=0), jnp.sum(value_grad, axis=0)])
    triple_half = jnp.stack([query_grad, key_grad, value_grad], axis=1).astype(jnp.bfloat16)
    triple_grad = jnp.einsum(
        "td,tcf->dcf", gathered, triple_half, preferred_element_type=jnp.float32
    )
    input_terms = jnp.einsum(
        "tcf,dcf->td", triple_half, triple_weight, preferred_element_type=jnp.float32
    )
    input_grad = first_grad + lax.psum_scatter(
        input_terms, "tensor", scatter_dimension=1, tiled=True
    )
    (
        triple_grad,
        query_value_grad,
        output_weight_grad,
        output_bias_grad,
        norm_gain_grad,
        norm_shift_grad,
        expand_weight_grad,
        expand_bias_grad,
        reduce_weight_grad,
        reduce_bias_grad,
        final_gain_grad,
        final_shift_grad,
    ) = lax.psum(
        (
            triple_grad,
            query_value_grad,
            output_weight_grad,
            output_bias_grad,
            norm_gain_grad,
            norm_shift_grad,
            expand_weight_grad,
            expand_bias_grad,
            reduce_weight_grad,
            reduce_bias_grad,
            final_gain_grad,
            final_shift_grad,
        ),
        "dp",
    )
    return (
        layer_output,
        input_grad,
        triple_grad,
        query_value_grad,
        output_weight_grad,
        output_bias_grad,
        norm_gain_grad,
        norm_shift_grad,
        expand_weight_grad,
        expand_bias_grad,
        reduce_weight_grad,
        reduce_bias_grad,
        final_gain_grad,
        final_shift_grad,
    )


def solution(mesh):
    in_specs = (
        P("dp", "tensor"),
        P("dp", None),
        P(None, None, "tensor"),
        P(None, "tensor"),
        P("tensor", None),
        P("tensor"),
        P("tensor"),
        P("tensor"),
        P(None, "tensor"),
        P("tensor"),
        P("tensor", None),
        P("tensor"),
        P("tensor"),
        P("tensor"),
        P("dp", "tensor"),
    )
    out_specs = (
        P("dp", "tensor"),
        P("dp", "tensor"),
        P(None, None, "tensor"),
        P(None, "tensor"),
        P("tensor", None),
        P("tensor"),
        P("tensor"),
        P("tensor"),
        P(None, "tensor"),
        P("tensor"),
        P("tensor", None),
        P("tensor"),
        P("tensor"),
        P("tensor"),
    )
    return jax.shard_map(
        per_device, mesh=mesh, in_specs=in_specs, out_specs=out_specs, check_vma=False
    )
```

profile of v0, /device:TPU:0, one launch (start us, length us, event | category | flops | bytes accessed | tf_op | source)
XLA Modules:
  0.0 474.9 jit_solution(481683990149905921)
XLA Ops:
  7.2 10.4 %all_gather.12 = bf16[512,768]{0,1:T(8,128)(2,1)S(1)} all-gather(bf16[512,192]{0,1:T(8,128)(2,1)} %param.15), channel_id=1, replica_groups=mesh['dp'=8,'tensor'=4] {'tensor'}, dimensions={1}, use_global_device_ids=true | all-gather | bytes 983040 | tf_op jit(solution)/shard_map/all_gather | solution.py:25
  17.7 1.8 fusion.41
  19.5 0.8 fusion.33
  20.7 0.8 fusion.1
  21.6 0.7 exponential_reduce_fusion
  22.3 0.9 copy-done.1
  23.2 1.0 convolution_convert_fusion.1
  24.3 1.6 fusion.37
  25.9 29.1 %reduce-scatter.5.cloned.1.call-done = f32[512,192]{0,1:T(8,128)} async-done(((f32[512,768]{0,1:T(8,128)}), f32[512,192]{0,1:T(8,128)}) %reduce-scatter.5.cloned.1.call-update) | async-done | bytes 393232 | tf_op jit(solution)/shard_map/reduce_scatter | solution.py:120
  55.0 1.1 fusion.30
  56.2 5.8 %all-reduce.5 = (f32[512]{0:T(512)S(1)}, f32[512]{0:T(512)S(1)}) all-reduce(f32[512]{0:T(512)S(1)} %get-tuple-element.23, f32[512]{0:T(512)S(1)} %get-tuple-element.22), channel_id=1, replica_groups=mesh['dp'=8,'tensor'=4] {'tensor'}, use_global_device_ids=true, to_apply=%region_6.7 | all-reduce | flops 1024 | bytes 8192 | tf_op jit(solution)/shard_map/psum | solution.py:29
  62.1 8.8 %all_gather.13 = bf16[512,768]{0,1:T(8,128)(2,1)S(1)} all-gather(bf16[512,192]{0,1:T(8,128)(2,1)S(1)} %fusion.20), channel_id=1, replica_groups=mesh['dp'=8,'tensor'=4] {'tensor'}, dimensions={1}, use_global_device_ids=true | all-gather | bytes 983040 | tf_op jit(solution)/shard_map/all_gather | solution.py:25
  70.8 0.9 copy-done.3
  71.7 2.1 multiply_convert_fusion.1
  73.8 0.9 copy-done.19
  74.7 2.0 fusion.38
  76.7 28.3 %reduce-scatter.7.cloned.1.call-done = f32[512,192]{0,1:T(8,128)} async-done(((f32[512,768]{0,1:T(8,128)}), f32[512,192]{0,1:T(8,128)}) %reduce-scatter.7.cloned.1.call-update) | async-done | bytes 393232 | tf_op jit(solution)/shard_map/reduce_scatter | solution.py:133
  105.0 1.2 fusion.29
  106.2 5.8 %all-reduce.4 = (f32[512]{0:T(512)S(1)}, f32[512]{0:T(512)S(1)}) all-reduce(f32[512]{0:T(512)S(1)} %get-tuple-element.21, f32[512]{0:T(512)S(1)} %get-tuple-element.20), channel_id=1, replica_groups=mesh['dp'=8,'tensor'=4] {'tensor'}, use_global_device_ids=true, to_apply=%region_11.12 | all-reduce | flops 1024 | bytes 8192 | tf_op jit(solution)/shard_map/psum | solution.py:29
  112.1 6.2 %all-reduce.3 = (f32[512]{0:T(512)}, f32[512]{0:T(512)S(1)}) all-reduce(f32[512]{0:T(512)S(1)} %get-tuple-element.25, f32[512]{0:T(512)S(1)} %get-tuple-element.24), channel_id=1, replica_groups=mesh['dp'=8,'tensor'=4] {'tensor'}, use_global_device_ids=true, to_apply=%region_15.16 | all-reduce | flops 1024 | bytes 8192 | tf_op jit(solution)/shard_map/psum | solution.py:29
  118.4 0.9 fusion.28
  119.3 8.9 %all_gather.14 = bf16[512,768]{0,1:T(8,128)(2,1)S(1)} all-gather(bf16[512,192]{0,1:T(8,128)(2,1)S(1)} %fusion.28), channel_id=1, replica_groups=mesh['dp'=8,'tensor'=4] {'tensor'}, dimensions={1}, use_global_device_ids=true | all-gather | bytes 983040 | tf_op jit(solution)/shard_map/all_gather | solution.py:25
  128.2 4.3 fusion.36
  132.5 3.1 fusion.18
  135.7 28.7 %reduce-scatter.9.cloned.1.call-done = f32[512,192]{0,1:T(8,128)} async-done(((f32[512,768]{0,1:T(8,128)}), f32[512,192]{0,1:T(8,128)}) %reduce-scatter.9.cloned.1.call-update) | async-done | bytes 393232 | tf_op jit(solution)/shard_map/reduce_scatter | solution.py:153
  164.4 2.7 fusion.14
  167.1 5.7 %all-reduce.2 = (f32[512]{0:T(512)S(1)}, f32[512]{0:T(512)S(1)}) all-reduce(f32[512]{0:T(512)S(1)} %get-tuple-element.58, f32[512]{0:T(512)S(1)} %get-tuple-element.57), channel_id=1, replica_groups=mesh['dp'=8,'tensor'=4] {'tensor'}, use_global_device_ids=true, to_apply=%region_20.21 | all-reduce | flops 1024 | bytes 8192 | tf_op jit(solution)/shard_map/psum | solution.py:29
  172.9 1.4 fusion.31
  174.3 9.1 %all_gather.15 = bf16[512,768]{0,1:T(8,128)(2,1)S(1)} all-gather(bf16[512,192]{0,1:T(8,128)(2,1)S(1)} %convert_element_type.69), channel_id=1, replica_groups=mesh['dp'=8,'tensor'=4] {'tensor'}, dimensions={1}, use_global_device_ids=true | all-gather | bytes 983040 | tf_op jit(solution)/shard_map/all_gather | solution.py:25
  183.4 1.3 convolution_convert_fusion.2
  184.8 1.1 fusion.35
  186.0 1.4 multiply_convert_fusion
  187.4 0.6 convolution_convert_fusion
  188.3 0.5 fusion.34
  188.9 2.0 convolution_bitcast_fusion.1
  191.0 3.7 fusion.16
  194.7 2.2 fusion.40
  197.0 1.2 fusion.39
  198.2 1.9 convolution_bitcast_fusion
  200.3 0.4 copy-done.40
  200.8 37.6 %all-reduce = (f32[2,192]{1,0:T(2,128)}, f32[192]{0:T(256)}, f32[192]{0:T(256)}, f32[192]{0:T(256)}, f32[768]{0:T(1024)}, /*index=5*/f32[192]{0:T(256)}, f32[192]{0:T(256)}, f32[192]{0:T(256)}) all-reduce(f32[2,192]{1,0:T(2,128)S(1)} %pad_maximum_fusion.3, f32[192]{0:T(256)S(1)} %get-tuple-element.49, ...), channel_id=1, replica_groups=mesh['dp'=8,'tensor'=4] {'dp'}, use_global_device_ids=true, to_apply=%region_25.26 | all-reduce | flops 2304 | bytes 18432 | tf_op jit(solution)/shard_map/psum | solution.py:221
  238.4 1.8 add.169
  240.2 220.4 %all-reduce.8.cloned.1.call-done = (f32[768,3,192]{0,2,1:T(8,128)}, f32[192,768]{1,0:T(8,128)}, f32[768,768]{1,0:T(8,128)}, f32[768,768]{1,0:T(8,128)}) async-done(((f32[768,3,192]{0,2,1:T(8,128)}, f32[192,768]{1,0:T(8,128)}, f32[768,768]{1,0:T(8,128)}, f32[768,768]{1,0:T(8,128)}), (f32[768,3,192]{0,2,1:T(8,128)}, f32[192,768]{1,0:T(8,128)}, f32[768,768]{1,0:T(8,128)}, ...) | async-done | bytes 7077904 | tf_op jit(solution)/shard_map/psum | solution.py:221
  460.7 2.9 copy.50
  463.6 0.8 copy.51
  464.4 1.4 copy.52
  465.9 1.1 copy-done.6
  467.0 1.4 copy.53
  (139 shorter events, 2.1 us)
Async XLA Ops:
  7.2 64.5 %copy-start = (bf16[768,768]{1,0:T(8,128)(2,1)S(1)}, bf16[768,768]{1,0:T(8,128)(2,1)}, u32[]{:S(2)}) copy-start(bf16[768,768]{1,0:T(8,128)(2,1)} %param.23) | copy-start | bytes 3538948
  7.2 47.8 %reduce-scatter.5.cloned.1.call-start = ((), (), s32[]{:S(2)}) async-start(), calls=%async_computation.4 | async-start | bytes 1966080 | tf_op jit(solution)/shard_map/reduce_scatter | solution.py:120
  20.3 1.2 copy-start.10
  20.4 1.9 copy-start.47
  20.6 1.7 copy-start.8
  21.5 1.7 copy-start.1
  21.6 1.7 copy-start.22
  22.3 1.9 copy-start.37
  24.2 1.6 copy-start.12
  24.2 30.8 %copy-start.18 = (bf16[512,192]{0,1:T(8,128)(2,1)S(1)}, bf16[512,192]{0,1:T(8,128)(2,1)}, u32[]{:S(2)}) copy-start(bf16[512,192]{0,1:T(8,128)(2,1)} %param.15) | copy-start | bytes 589828
  24.3 30.8 %copy-start.50 = (f32[192]{0:T(256)S(1)}, f32[192]{0:T(256)}, u32[]{:S(2)}) copy-start(f32[192]{0:T(256)} %param.20) | copy-start | bytes 2308
  25.8 36.1 %copy-start.32 = (f32[192]{0:T(256)S(1)}, f32[192]{0:T(256)}, u32[]{:S(2)}) copy-start(f32[192]{0:T(256)} %param.21) | copy-start | bytes 2308
  25.8 36.1 %copy-start.46 = (f32[192]{0:T(256)S(1)}, f32[192]{0:T(256)}, u32[]{:S(2)}) copy-start(f32[192]{0:T(256)} %param.22) | copy-start | bytes 2308
  25.9 45.9 %copy-start.55 = (f32[768]{0:T(1024)S(1)}, f32[768]{0:T(1024)}, u32[]{:S(2)}) copy-start(f32[768]{0:T(1024)} %param.24) | copy-start | bytes 9220
  25.9 79.1 %reduce-scatter.7.cloned.1.call-start = ((), (), s32[]{:S(2)}) async-start(), calls=%async_computation.5 | async-start | bytes 1966080 | tf_op jit(solution)/shard_map/reduce_scatter | solution.py:133
  71.7 2.9 copy-start.53
  76.6 28.4 %copy-start.52 = (f32[192]{0:T(256)S(1)}, f32[192]{0:T(256)}, u32[]{:S(2)}) copy-start(f32[192]{0:T(256)} %param.26) | copy-start | bytes 2308
  76.6 35.3 %copy-start.15 = (bf16[512,192]{0,1:T(8,128)(2,1)S(1)}, bf16[512,192]{0,1:T(8,128)(2,1)}, u32[]{:S(2)}) copy-start(bf16[512,192]{0,1:T(8,128)(2,1)} %param.29) | copy-start | bytes 589828
  76.6 35.3 %copy-start.34 = (f32[192]{0:T(256)S(1)}, f32[192]{0:T(256)}, u32[]{:S(2)}) copy-start(f32[192]{0:T(256)} %param.27) | copy-start | bytes 2308
  76.7 87.7 %reduce-scatter.9.cloned.1.call-start = ((), (), s32[]{:S(2)}) async-start(), calls=%async_computation.6 | async-start | bytes 1966080 | tf_op jit(solution)/shard_map/reduce_scatter | solution.py:153
  118.4 9.8 %copy-start.54 = (bf16[768,768]{1,0:T(8,128)(2,1)S(1)}, bf16[768,768]{1,0:T(8,128)(2,1)}, u32[]{:S(2)}) copy-start(bf16[768,768]{1,0:T(8,128)(2,1)} %param.25) | copy-start | bytes 3538948
  118.4 9.8 %copy-start.30 = (f32[512]{0:T(512)}, f32[512]{0:T(512)S(1)}, u32[]{:S(2)}) copy-start(f32[512]{0:T(512)S(1)} %broadcast_multiply_fusion.1) | copy-start | bytes 6148
  128.2 4.3 copy-start.4
  135.6 28.8 %copy-start.31 = (f32[512]{0:T(512)S(1)}, f32[512]{0:T(512)}, u32[]{:S(2)}) copy-start(f32[512]{0:T(512)} %copy-done.30) | copy-start | bytes 6148
  135.6 28.8 %copy-start.33 = (f32[192]{0:T(256)S(1)}, f32[192]{0:T(256)}, u32[]{:S(2)}) copy-start(f32[192]{0:T(256)} %param.21) | copy-start | bytes 2308
  135.6 28.8 %copy-start.35 = (f32[192]{0:T(256)S(1)}, f32[192]{0:T(256)}, u32[]{:S(2)}) copy-start(f32[192]{0:T(256)} %param.27) | copy-start | bytes 2308
  135.6 28.8 %copy-start.39 = (f32[512]{0:T(512)S(1)}, f32[512]{0:T(512)}, u32[]{:S(2)}) copy-start(f32[512]{0:T(512)} %get-tuple-element.43) | copy-start | bytes 6148
  135.6 28.8 %copy-start.51 = (f32[192]{0:T(256)S(1)}, f32[192]{0:T(256)}, u32[]{:S(2)}) copy-start(f32[192]{0:T(256)} %param.28) | copy-start | bytes 2308
  135.6 102.8 %reduce-scatter.11.cloned.1.call-start = ((), (), s32[]{:S(2)}) async-start(), calls=%async_computation.7 | async-start | bytes 1966080 | tf_op jit(solution)/shard_map/reduce_scatter | solution.py:205
  172.9 11.8 %copy-start.2 = (f32[3,512,512]{1,2,0:T(8,128)S(1)}, f32[3,512,512]{1,2,0:T(8,128)}, u32[]{:S(2)}) copy-start(f32[3,512,512]{1,2,0:T(8,128)} %copy-done.1) | copy-start | bytes 9437188
  174.3 10.4 %copy-start.9 = (pred[512,512]{0,1:T(8,128)(4,1)S(1)}, pred[512,512]{0,1:T(8,128)(4,1)}, u32[]{:S(2)}) copy-start(pred[512,512]{0,1:T(8,128)(4,1)} %copy-done.8) | copy-start | bytes 786436
  174.3 10.4 %copy-start.38 = (f32[3,512]{1,0:T(4,128)S(1)}, f32[3,512]{1,0:T(4,128)}, u32[]{:S(2)}) copy-start(f32[3,512]{1,0:T(4,128)} %copy-done.37) | copy-start | bytes 18436
  184.7 1.2 copy-start.23
  184.7 1.2 copy-start.48
  185.8 2.9 copy-start.56
  185.9 1.4 copy-start.29
  187.3 1.6 copy-start.17
  188.7 2.2 copy-start.26
  191.0 269.7 %all-reduce.8.cloned.1.call-start = ((), (), s32[]{:S(2)}) async-start(), calls=%async_computation.8 | async-start | bytes 14155776 | tf_op jit(solution)/shard_map/psum | solution.py:221
  191.0 3.7 copy-start.5
  191.0 3.7 copy-start.20
  194.7 2.2 copy-start.14
  196.9 1.2 copy-start.25
  196.9 1.2 copy-start.27
  196.9 1.2 copy-start.57
  460.7 3.0 copy-start.21
  460.7 3.8 copy-start.7
  464.4 2.5 copy-start.6
  (15 other events, 12.4 us)
Sparse Core Ops, SparseCore 0:
  26.0 29.0 reduce-scatter.4
  76.8 28.1 reduce-scatter.6
  135.7 28.6 reduce-scatter.8
  191.1 28.1 reduce-scatter.10
  224.7 235.8 all-reduce.7
where the time goes:
time: 476 us; the launch traced here: 475 us
  waiting for transfers between devices  307 us (64%)
  blocking collectives  98.2 us (21%)
  matrix products  32.3 us (7%)
  between operations  14.3 us (3%)
  local copies, waits for them, and re-layouts  12.8 us (3%)
  other arithmetic  10.5 us (2%)
    psum x1, waiting for transfers between devices, per_device(): lax.psum((triple_grad, query_value_grad, output_weight_grad, output_bias_...  220 us
    psum x1, blocking collectives, per_device(): lax.psum((triple_grad, query_value_grad, output_weight_grad, output_bias_...  37.6 us
    all_gather x4, blocking collectives, widen(): return lax.all_gather(piece, 'tensor', axis=1, tiled=True)  37.1 us
    reduce_scatter x1, waiting for transfers between devices, per_device(): lax.psum_scatter(jnp.dot(context_flat, output_weight, preferred_element_t...  29.1 us
    reduce_scatter x1, waiting for transfers between devices, per_device(): lax.psum_scatter(wide_dot(act_half, expand_weight), 'tensor', scatter_dim...  28.7 us
    reduce_scatter x1, waiting for transfers between devices, per_device(): lax.psum_scatter(jnp.dot(activated, reduce_weight, preferred_element_type...  28.3 us
    psum x4, blocking collectives, row_stats(): return lax.psum((jnp.sum(first, axis=1), jnp.sum(second, axis=1)), 'tensor')  23.5 us
    unnamed x120, local copies, waits for them, and re-layouts  11.6 us
  transfers between devices with their start and end apart: 5, of which 4 were waited for; matrix products, arithmetic and copies ran while one was open for 2% of the time, Pallas kernels for 0%

commit v1 on v0

v1 whole, which is shorter than its diff:
```python
import jax
import jax.numpy as jnp
from jax import lax
from jax.sharding import PartitionSpec as P

D = 768
HD = 64


EPS = 1e-06


def gelu_value(pre_act):
    return 0.5 * pre_act * (1.0 + lax.erf(pre_act * 0.7071067811865476))


def gelu_slope(pre_act):
    return (
        0.5 * (1.0 + lax.erf(pre_act * 0.7071067811865476))
        + pre_act * jnp.exp(-0.5 * pre_act * pre_act) * 0.3989422804014327
    )


def norm_forward(hidden, gain, shift):
    row_mean = jnp.mean(hidden, axis=-1, keepdims=True)
    centred = hidden - row_mean
    inverse = lax.rsqrt(jnp.mean(centred * centred, axis=-1, keepdims=True) + EPS)
    normed = centred * inverse
    return (normed * gain + shift, normed, inverse)


def norm_backward(upstream, normed, inverse, gain):
    scaled = upstream * gain
    first_mean = jnp.mean(scaled, axis=-1, keepdims=True)
    second_mean = jnp.mean(scaled * normed, axis=-1, keepdims=True)
    return inverse * (scaled - first_mean - normed * second_mean)


def sum_rows(partial):
    return lax.psum_scatter(
        partial.astype(jnp.bfloat16), "tensor", scatter_dimension=0, tiled=True
    ).astype(jnp.float32)


def all_rows(piece):
    return lax.all_gather(piece, "tensor", axis=0, tiled=True)


def column_sum(rows):
    return jnp.sum(rows, axis=0)


def tall_dot(left, right):
    return lax.dot_general(
        left, right, (((0,), (0,)), ((), ())), preferred_element_type=jnp.float32
    )


def wide_dot(left, right):
    return lax.dot_general(
        left, right, (((1,), (1,)), ((), ())), preferred_element_type=jnp.float32
    )


def masked_scores(query_part, key_part, segment_row, head_scale):
    scores = (
        jnp.einsum("qhd,khd->hqk", query_part, key_part, preferred_element_type=jnp.float32)
        * head_scale
    )
    allowed = segment_row[:, None] == segment_row[None, :]
    return jnp.where(allowed[None], scores, -jnp.inf)


def per_device(
    layer_input,
    segment_ids,
    triple_weight,
    query_value_bias,
    output_weight,
    output_bias,
    norm_gain,
    norm_shift,
    expand_weight,
    expand_bias,
    reduce_weight,
    reduce_bias,
    final_gain,
    final_shift,
    cotangent,
):
    seq_len = segment_ids.shape[1]
    tok_count = segment_ids.shape[0] * seq_len
    local_width = triple_weight.shape[2]
    local_heads = local_width // HD
    head_scale = HD ** (-0.5)
    groups = lax.axis_size("tensor")
    rank = lax.axis_index("tensor")
    block = tok_count // groups
    both = lax.all_gather(
        jnp.concatenate([layer_input, cotangent], axis=0), "tensor", axis=1, tiled=True
    )
    gathered = both[:tok_count]
    own_input = lax.dynamic_slice_in_dim(both, rank * block, block, 0).astype(jnp.float32)
    upstream = lax.dynamic_slice_in_dim(both, tok_count + rank * block, block, 0).astype(
        jnp.float32
    )
    vectors = lax.all_gather(
        jnp.stack([output_bias, norm_gain, norm_shift, reduce_bias, final_gain, final_shift]),
        "tensor",
        axis=1,
        tiled=True,
    )
    output_bias, norm_gain, norm_shift, reduce_bias, final_gain, final_shift = [
        vectors[i] for i in range(6)
    ]
    projected = jnp.einsum(
        "td,dcf->tcf", gathered, triple_weight, preferred_element_type=jnp.float32
    )
    query_half = (
        (projected[:, 0] + query_value_bias[0])
        .astype(jnp.bfloat16)
        .reshape(seq_len, local_heads, HD)
    )
    key_half = projected[:, 1].astype(jnp.bfloat16).reshape(seq_len, local_heads, HD)
    value_half = (
        (projected[:, 2] + query_value_bias[1])
        .astype(jnp.bfloat16)
        .reshape(seq_len, local_heads, HD)
    )
    scores = masked_scores(query_half, key_half, segment_ids[0], head_scale)
    top = jnp.max(scores, axis=-1, keepdims=True)
    log_total = top + jnp.log(jnp.sum(jnp.exp(scores - top), axis=-1, keepdims=True))
    probs_half = jnp.exp(scores - log_total).astype(jnp.bfloat16)
    context = jnp.einsum(
        "hqk,khd->qhd", probs_half, value_half, preferred_element_type=jnp.float32
    ).astype(jnp.bfloat16)
    context_flat = context.reshape(tok_count, local_width)
    first_sum = (
        own_input
        + sum_rows(jnp.dot(context_flat, output_weight, preferred_element_type=jnp.float32))
        + output_bias
    )
    attended, normed_one, inv_one = norm_forward(first_sum, norm_gain, norm_shift)
    attended_half = all_rows(attended.astype(jnp.bfloat16))
    pre_act = (
        jnp.dot(attended_half, expand_weight, preferred_element_type=jnp.float32) + expand_bias
    )
    activated = gelu_value(pre_act).astype(jnp.bfloat16)
    second_sum = (
        attended
        + sum_rows(jnp.dot(activated, reduce_weight, preferred_element_type=jnp.float32))
        + reduce_bias
    )
    out_f, normed_two, inv_two = norm_forward(second_sum, final_gain, final_shift)
    layer_output = lax.all_to_all(
        out_f.astype(jnp.bfloat16), "tensor", split_axis=1, concat_axis=0, tiled=True
    )
    final_gain_grad = column_sum(upstream * normed_two)
    final_shift_grad = column_sum(upstream)
    second_grad = norm_backward(upstream, normed_two, inv_two, final_gain)
    second_half = all_rows(second_grad.astype(jnp.bfloat16))
    reduce_weight_grad = tall_dot(activated, second_half)
    reduce_bias_grad = column_sum(second_grad)
    act_grad = wide_dot(second_half, reduce_weight) * gelu_slope(pre_act)
    act_half = act_grad.astype(jnp.bfloat16)
    expand_weight_grad = tall_dot(attended_half, act_half)
    expand_bias_grad = column_sum(act_grad)
    feed_sum = lax.psum(
        jnp.concatenate([reduce_weight_grad, expand_weight_grad], axis=0).astype(jnp.bfloat16),
        "dp",
    )
    split = reduce_weight_grad.shape[0]
    attended_grad = second_grad + sum_rows(wide_dot(act_half, expand_weight))
    norm_gain_grad = column_sum(attended_grad * normed_one)
    norm_shift_grad = column_sum(attended_grad)
    first_grad = norm_backward(attended_grad, normed_one, inv_one, norm_gain)
    first_half = all_rows(first_grad.astype(jnp.bfloat16))
    output_weight_grad = tall_dot(context_flat, first_half)
    output_bias_grad = column_sum(first_grad)
    grad_part = (
        wide_dot(first_half, output_weight)
        .astype(jnp.bfloat16)
        .reshape(seq_len, local_heads, HD)
    )
    scores = masked_scores(query_half, key_half, segment_ids[0], head_scale)
    probs = jnp.exp(scores - log_total)
    probs_half = probs.astype(jnp.bfloat16)
    value_grad = jnp.einsum(
        "hqk,qhd->khd", probs_half, grad_part, preferred_element_type=jnp.float32
    ).reshape(tok_count, local_width)
    prob_grad = jnp.einsum(
        "qhd,khd->hqk", grad_part, value_half, preferred_element_type=jnp.float32
    )
    delta = jnp.einsum(
        "qhd,qhd->hq", grad_part.astype(jnp.float32), context.astype(jnp.float32)
    )
    score_grad = (probs * (prob_grad - delta[:, :, None]) * head_scale).astype(jnp.bfloat16)
    query_grad = jnp.einsum(
        "hqk,khd->qhd", score_grad, key_half, preferred_element_type=jnp.float32
    ).reshape(tok_count, local_width)
    key_grad = jnp.einsum(
        "hqk,qhd->khd", score_grad, query_half, preferred_element_type=jnp.float32
    ).reshape(tok_count, local_width)
    triple_half = jnp.stack([query_grad, key_grad, value_grad], axis=1).astype(jnp.bfloat16)
    triple_grad = jnp.einsum(
        "td,tcf->dcf", gathered, triple_half, preferred_element_type=jnp.float32
    )
    input_terms = jnp.einsum(
        "tcf,dcf->td", triple_half, triple_weight, preferred_element_type=jnp.float32
    )
    smalls = jnp.stack(
        [
            output_bias_grad,
            norm_gain_grad,
            norm_shift_grad,
            reduce_bias_grad,
            final_gain_grad,
            final_shift_grad,
        ]
    )
    own_rows = lax.dynamic_slice_in_dim(input_terms, rank * block, block, 0) + first_grad
    input_terms = lax.dynamic_update_slice_in_dim(input_terms, own_rows, rank * block, 0)
    shares = lax.psum_scatter(
        jnp.concatenate([input_terms, smalls, jnp.zeros((10, D), jnp.float32)], axis=0).astype(jnp.bfloat16),
        "tensor",
        scatter_dimension=1,
        tiled=True,
    ).astype(jnp.float32)
    input_grad = shares[:tok_count]
    pieces = [
        triple_grad,
        output_weight_grad,
        expand_bias_grad,
        jnp.sum(query_grad, axis=0),
        jnp.sum(value_grad, axis=0),
        shares[tok_count : tok_count + 6],
    ]
    packed = jnp.concatenate([p.reshape(-1, local_width) for p in pieces], axis=0)
    packed, feed_sum = lax.optimization_barrier((packed.astype(jnp.bfloat16), feed_sum))
    packed = lax.psum(packed, "dp").astype(jnp.float32)
    reduce_weight_grad = feed_sum[:split].astype(jnp.float32)
    expand_weight_grad = feed_sum[split:].astype(jnp.float32)
    outs, at = [], 0
    for p in pieces:
        count = p.size // local_width
        outs.append(packed[at : at + count].reshape(p.shape))
        at += count
    triple_grad, output_weight_grad, expand_bias_grad, query_sum, value_sum, small_sums = outs
    return (
        layer_output,
        input_grad,
        triple_grad,
        jnp.stack([query_sum, value_sum]),
        output_weight_grad,
        small_sums[0],
        small_sums[1],
        small_sums[2],
        expand_weight_grad,
        expand_bias_grad,
        reduce_weight_grad,
        small_sums[3],
        small_sums[4],
        small_sums[5],
    )


def solution(mesh):
    in_specs = (
        P("dp", "tensor"),
        P("dp", None),
        P(None, None, "tensor"),
        P(None, "tensor"),
        P("tensor", None),
        P("tensor"),
        P("tensor"),
        P("tensor"),
        P(None, "tensor"),
        P("tensor"),
        P("tensor", None),
        P("tensor"),
        P("tensor"),
        P("tensor"),
        P("dp", "tensor"),
    )
    out_specs = (
        P("dp", "tensor"),
        P("dp", "tensor"),
        P(None, None, "tensor"),
        P(None, "tensor"),
        P("tensor", None),
        P("tensor"),
        P("tensor"),
        P("tensor"),
        P(None, "tensor"),
        P("tensor"),
        P("tensor", None),
        P("tensor"),
        P("tensor"),
        P("tensor"),
    )
    return jax.shard_map(
        per_device, mesh=mesh, in_specs=in_specs, out_specs=out_specs, check_vma=False
    )
```

time: 476 us -> 415 us (0.87)
  blocking collectives: 98.2 us -> 38.8 us
  waiting for transfers between devices: 307 us -> 275 us
  local copies, waits for them, and re-layouts: 12.8 us -> 41.6 us
  other arithmetic: 10.5 us -> 20.5 us
  matrix products: 32.3 us -> 22.5 us
    psum x5 -> x0, blocking collectives: 61.1 us -> none  [the longest x1 37.6 us: per_device(): lax.psum((triple_grad, query_value_grad, output_weight_grad, output_bias_...]
    psum x1 -> x2, waiting for transfers between devices: 220 us -> 180 us  [the longest x1 105 us: per_device(): lax.psum(jnp.concatenate([reduce_weight_grad, expand_weight_grad], axis=0...]
    reduce_scatter x4 -> x3, waiting for transfers between devices: 86.1 us -> 63.9 us  [sum_rows(): lax.psum_scatter(partial.astype(jnp.bfloat16), 'tensor', scatter_dimensio...]
    all_gather x0 -> x1, waiting for transfers between devices: none -> 21.4 us  [per_device(): lax.all_gather(jnp.concatenate([layer_input, cotangent], axis=0), 'tensor...]
    unnamed x5 -> x8, waiting for transfers between devices: 0.08 us -> 10.1 us
    concatenate x0 -> x2, local copies, waits for them, and re-layouts: none -> 9.81 us  [the longest x1 6.74 us: per_device(): jnp.concatenate([p.reshape(-1, local_width) for p in pieces], axis=0)]
    all_to_all x0 -> x1, blocking collectives: none -> 8.67 us  [per_device(): lax.all_to_all(out_f.astype(jnp.bfloat16), 'tensor', split_axis=1, concat...]
    reshape x0 -> x8, local copies, waits for them, and re-layouts: none -> 7.21 us  [the longest x3 4.38 us: per_device(): outs.append(packed[at:at + count].reshape(p.shape))]
  transfers between devices with their start and end apart: 5 -> 7, of which waited for: 4 -> 7; matrix products, arithmetic and copies ran while one was open for 2% -> 9% of each run, Pallas kernels for 0% -> 0%
where the time goes in v1:
time: 415 us; the launch traced here: 414 us
  waiting for transfers between devices  275 us (66%)
  local copies, waits for them, and re-layouts  41.6 us (10%)
  blocking collectives  38.8 us (9%)
  matrix products  22.5 us (5%)
  other arithmetic  20.5 us (5%)
  between operations  14.7 us (4%)
    psum x1, waiting for transfers between devices, per_device(): lax.psum(jnp.concatenate([reduce_weight_grad, expand_weight_grad], axis=0...  105 us
    psum x1, waiting for transfers between devices, per_device(): packed = lax.psum(packed, 'dp').astype(jnp.float32)  74.8 us
    reduce_scatter x3, waiting for transfers between devices, sum_rows(): lax.psum_scatter(partial.astype(jnp.bfloat16), 'tensor', scatter_dimensio...  63.9 us
    all_gather x3, blocking collectives, all_rows(): return lax.all_gather(piece, 'tensor', axis=0, tiled=True)  24.9 us
    all_gather x1, waiting for transfers between devices, per_device(): lax.all_gather(jnp.concatenate([layer_input, cotangent], axis=0), 'tensor...  21.4 us
    unnamed x76, local copies, waits for them, and re-layouts  13.2 us
    unnamed x8, waiting for transfers between devices  10.1 us
    all_to_all x1, blocking collectives, per_device(): lax.all_to_all(out_f.astype(jnp.bfloat16), 'tensor', split_axis=1, concat...  8.67 us
  transfers between devices with their start and end apart: 7, of which 7 were waited for; matrix products, arithmetic and copies ran while one was open for 9% of the time, Pallas kernels for 0%

profile of v1, /device:TPU:0, one launch (start us, length us, event | category | flops | bytes accessed | tf_op | source)
XLA Modules:
  0.0 413.7 jit_solution(5651966376495020116)
XLA Ops:
  7.2 1.9 pad_maximum_fusion.2
  11.1 21.4 %all-gather.3.cloned.1.call-done = bf16[1024,768]{0,1:T(8,128)(2,1)} async-done(((bf16[1024,192]{0,1:T(8,128)(2,1)}), bf16[1024,768]{0,1:T(8,128)(2,1)}) %all-gather.3.cloned.1.call-update) | async-done | bytes 1572880 | tf_op jit(solution)/shard_map/all_gather | solution.py:99
  32.6 2.0 fusion.7
  37.1 1.0 convolution_convert_fusion.7
  38.2 1.3 convolution_convert_fusion.4
  39.7 5.2 %all-gather = f32[4,192,6]{1,2,0:T(8,128)S(1)} all-gather(f32[1,192,6]{1,2,0:T(8,128)S(1)} %bitcast.109), channel_id=1, replica_groups=mesh['dp'=8,'tensor'=4] {'tensor'}, dimensions={0}, use_global_device_ids=true | all-gather | bytes 23040 | tf_op jit(solution)/shard_map/all_gather | solution.py:107
  45.0 1.2 fusion.27
  46.4 16.6 %reduce-scatter.7.cloned.1.call-done = bf16[128,768]{1,0:T(8,128)(2,1)} async-done(((bf16[512,768]{1,0:T(8,128)(2,1)}), bf16[128,768]{1,0:T(8,128)(2,1)}) %reduce-scatter.7.cloned.1.call-update) | async-done | bytes 196624 | tf_op jit(solution)/shard_map/reduce_scatter | solution.py:40
  63.0 1.1 fusion.22
  64.0 1.1 multiply_reduce_fusion.3
  65.2 1.1 fusion.21
  66.2 8.2 %all_gather.17 = bf16[512,768]{1,0:T(8,128)(2,1)S(1)} all-gather(bf16[128,768]{1,0:T(8,128)(2,1)S(1)} %fusion.21), channel_id=1, replica_groups=mesh['dp'=8,'tensor'=4] {'tensor'}, dimensions={0}, use_global_device_ids=true | all-gather | bytes 983040 | tf_op jit(solution)/shard_map/all_gather | solution.py:46
  74.5 2.0 multiply_convert_fusion.1
  77.4 1.7 convolution_convert_fusion.3
  79.3 23.6 %reduce-scatter.9.cloned.1.call-done = bf16[128,768]{1,0:T(8,128)(2,1)} async-done(((bf16[512,768]{1,0:T(8,128)(2,1)}), bf16[128,768]{1,0:T(8,128)(2,1)}) %reduce-scatter.9.cloned.1.call-update) | async-done | bytes 196624 | tf_op jit(solution)/shard_map/reduce_scatter | solution.py:40
  102.9 1.2 fusion.31
  105.5 8.2 %all_gather.18 = bf16[512,768]{1,0:T(8,128)(2,1)S(1)} all-gather(bf16[128,768]{1,0:T(8,128)(2,1)S(1)} %get-tuple-element.94), channel_id=1, replica_groups=mesh['dp'=8,'tensor'=4] {'tensor'}, dimensions={0}, use_global_device_ids=true | all-gather | bytes 983040 | tf_op jit(solution)/shard_map/all_gather | solution.py:46
  113.7 1.7 fusion.36
  116.2 1.7 convolution_convert_fusion.2
  118.0 23.7 %reduce-scatter.11.cloned.1.call-done = bf16[128,768]{1,0:T(8,128)(2,1)} async-done(((bf16[512,768]{1,0:T(8,128)(2,1)}), bf16[128,768]{1,0:T(8,128)(2,1)}) %reduce-scatter.11.cloned.1.call-update) | async-done | bytes 196624 | tf_op jit(solution)/shard_map/reduce_scatter | solution.py:40
  141.8 1.3 multiply_reduce_fusion
  143.1 1.2 fusion.28
  144.3 8.5 %all_gather.19 = bf16[512,768]{1,0:T(8,128)(2,1)S(1)} all-gather(bf16[128,768]{1,0:T(8,128)(2,1)S(1)} %convert_element_type.106), channel_id=1, replica_groups=mesh['dp'=8,'tensor'=4] {'tensor'}, dimensions={0}, use_global_device_ids=true | all-gather | bytes 983040 | tf_op jit(solution)/shard_map/all_gather | solution.py:46
  153.4 1.4 multiply_convert_fusion
  155.8 1.7 fusion.34
  159.4 3.1 concatenate.16
  162.5 1.3 copy.87
  163.9 2.3 convolution_convert_fusion.1
  167.0 1.6 pad_maximum_fusion
  169.4 1.2 pad_maximum_fusion.1
  171.2 1.0 convert.85
  172.2 2.5 copy.72
  174.8 2.2 reshape.172
  177.0 1.3 convolution_convert_fusion.5
  178.9 10.0 %reduce-scatter.13.cloned.1.call-done = bf16[192,528]{1,0:T(8,128)(2,1)} async-done(((bf16[768,528]{1,0:T(8,128)(2,1)}), bf16[192,528]{1,0:T(8,128)(2,1)}) %reduce-scatter.13.cloned.1.call-update) | async-done | bytes 202768
  189.8 6.7 %concatenate.17 = bf16[3084,192]{1,0:T(8,128)(2,1)} concatenate(bf16[2304,192]{1,0:T(8,128)(2,1)S(1)} %copy-done.5, bf16[768,192]{1,0:T(8,128)(2,1)S(1)} %reshape.173, bf16[4,192]{1,0:T(4,128)(2,1)S(1)} %reshape.174, bf16[1,192]{1,0:T(2,128)(2,1)S(1)} %reshape.175, bf16[1,192]{1,0:T(2,128)(2,1)S(1)} %reshape.176, bf16[6,192]{1,0:T(8,128)(2,1)S(1)} %copy.93), dimensions={0} | concatenate | bytes 2368512 | tf_op jit(solution)/shard_map/concatenate | solution.py:238
  196.5 105.1 %all-reduce.3.cloned.1.call-done = bf16[1536,768]{1,0:T(8,128)(2,1)} async-done(((bf16[1536,768]{1,0:T(8,128)(2,1)}), bf16[1536,768]{1,0:T(8,128)(2,1)}) %all-reduce.3.cloned.1.call-update) | async-done | bytes 2359312 | tf_op jit(solution)/shard_map/psum | solution.py:168
  301.7 1.9 copy.65
  303.6 8.7 %all_to_all.19 = bf16[128,4,192]{0,2,1:T(8,128)(2,1)S(1)} all-to-all(bf16[128,4,192]{0,2,1:T(8,128)(2,1)} %bitcast.101), channel_id=1, replica_groups=mesh['dp'=8,'tensor'=4] {'tensor'}, dimensions={1} | all-to-all | bytes 393216 | tf_op jit(solution)/shard_map/all_to_all | solution.py:155
  312.9 1.6 slice.126
  314.5 1.8 copy.92
  316.3 1.8 copy.73
  318.1 2.5 slice_convert_fusion
  320.7 74.8 %all-reduce.5.cloned.1.call-done = bf16[3084,192]{1,0:T(8,128)(2,1)} async-done(((bf16[3084,192]{1,0:T(8,128)(2,1)}), bf16[3084,192]{1,0:T(8,128)(2,1)}) %all-reduce.5.cloned.1.call-update) | async-done | bytes 1184272 | tf_op jit(solution)/shard_map/psum | solution.py:240
  395.5 1.4 slice.128
  396.9 2.6 reshape.177
  399.5 4.3 %copy.74 = f32[768,3,192]{0,2,1:T(8,128)} copy(f32[768,3,192]{2,1,0:T(4,128)} %reshape.177) | data formatting | bytes 3538944
  403.9 1.1 reshape.178
  (136 shorter events, 18.3 us)
Async XLA Ops:
  7.2 67.3 %copy-start = (bf16[768,768]{1,0:T(8,128)(2,1)S(1)}, bf16[768,768]{1,0:T(8,128)(2,1)}, u32[]{:S(2)}) copy-start(bf16[768,768]{1,0:T(8,128)(2,1)} %param.23) | copy-start | bytes 3538948
  7.2 25.4 %all-gather.3.cloned.1.call-start = ((), (), s32[]{:S(2)}) async-start(), calls=%async_computation.5 | async-start | bytes 1966080 | tf_op jit(solution)/shard_map/all_gather | solution.py:99
  9.2 53.8 %reduce-scatter.7.cloned.1.call-start = ((), (), s32[]{:S(2)}) async-start(), calls=%async_computation.6 | async-start | bytes 983040 | tf_op jit(solution)/shard_map/reduce_scatter | solution.py:40
  34.6 1.6 copy-start.16
  35.5 1.7 copy-start.1
  37.1 1.1 copy-start.9
  38.1 115.1 %copy-start.8 = (bf16[3,64,512]{2,1,0:T(8,128)(2,1)}, bf16[3,64,512]{2,1,0:T(8,128)(2,1)S(1)}, u32[]{:S(2)}) copy-start(bf16[3,64,512]{2,1,0:T(8,128)(2,1)S(1)} %convolution_convert_fusion.7) | copy-start | bytes 589828
  38.1 1.5 copy-start.20
  38.2 1.5 copy-start.21
  38.2 1.5 copy-start.22
  38.2 1.4 copy-start.23
  38.2 1.4 copy-start.24
  38.2 1.4 copy-start.25
  39.5 63.4 %reduce-scatter.9.cloned.1.call-start = ((), (), s32[]{:S(2)}) async-start(), calls=%async_computation.7 | async-start | bytes 983040 | tf_op jit(solution)/shard_map/reduce_scatter | solution.py:40
  46.2 28.2 %copy-start.29 = (f32[768]{0:T(1024)S(1)}, f32[768]{0:T(1024)}, u32[]{:S(2)}) copy-start(f32[768]{0:T(1024)} %param.24) | copy-start | bytes 9220
  74.5 2.0 copy-start.13
  74.5 3.0 copy-start.27
  76.5 0.9 copy-start.30
  77.4 25.5 %copy-start.3 = (bf16[128,768]{1,0:T(8,128)(2,1)S(1)}, bf16[128,768]{1,0:T(8,128)(2,1)}, u32[]{:S(2)}) copy-start(bf16[128,768]{1,0:T(8,128)(2,1)} %reduce-scatter.7.cloned.1.call-done) | copy-start | bytes 589828
  79.1 62.7 %reduce-scatter.11.cloned.1.call-start = ((), (), s32[]{:S(2)}) async-start(), calls=%async_computation.8 | async-start | bytes 983040 | tf_op jit(solution)/shard_map/reduce_scatter | solution.py:40
  104.3 9.4 %copy-start.28 = (bf16[768,768]{1,0:T(8,128)(2,1)S(1)}, bf16[768,768]{1,0:T(8,128)(2,1)}, u32[]{:S(2)}) copy-start(bf16[768,768]{1,0:T(8,128)(2,1)} %param.25) | copy-start | bytes 3538948
  104.3 9.4 %copy-start.33 = (f32[512,768]{1,0:T(8,128)S(1)}, f32[512,768]{1,0:T(8,128)}, u32[]{:S(2)}) copy-start(f32[512,768]{1,0:T(8,128)} %get-tuple-element.117) | copy-start | bytes 4718596
  113.7 1.7 copy-start.15
  115.4 0.9 copy-start.31
  118.0 70.9 %reduce-scatter.13.cloned.1.call-start = ((), (), s32[]{:S(2)}) async-start(), calls=%async_computation.11 | async-start | bytes 1228800
  143.1 10.3 %copy-start.17 = (f32[512,1,192]{0,2,1:T(8,128)S(1)}, f32[512,1,192]{0,2,1:T(8,128)}, u32[]{:S(2)}) copy-start(f32[512,1,192]{0,2,1:T(8,128)} %copy-done.16) | copy-start | bytes 1179652
  144.3 9.1 %copy-start.2 = (f32[3,512,512]{1,2,0:T(8,128)S(1)}, f32[3,512,512]{1,2,0:T(8,128)}, u32[]{:S(2)}) copy-start(f32[3,512,512]{1,2,0:T(8,128)} %copy-done.1) | copy-start | bytes 9437188
  155.2 2.3 copy-start.11
  155.8 1.7 copy-start.12
  155.8 1.7 copy-start.10
  157.5 0.8 copy-start.18
  163.8 2.4 copy-start.14
  163.9 2.4 copy-start.32
  163.9 137.8 %all-reduce.3.cloned.1.call-start = ((), (), s32[]{:S(2)}) async-start(), calls=%async_computation.9 | async-start | bytes 4718592 | tf_op jit(solution)/shard_map/psum | solution.py:168
  168.6 0.7 copy-start.19
  168.6 2.0 copy-start.6
  168.6 226.9 %all-reduce.5.cloned.1.call-start = ((), (), s32[]{:S(2)}) async-start(), calls=%async_computation.10 | async-start | bytes 3162112 | tf_op jit(solution)/shard_map/psum | solution.py:240
  177.0 1.8 copy-start.26
  177.0 12.8 %copy-start.5 = (bf16[2304,192]{1,0:T(8,128)(2,1)S(1)}, bf16[2304,192]{1,0:T(8,128)(2,1)}, u32[]{:S(2)}) copy-start(bf16[2304,192]{1,0:T(8,128)(2,1)} %reshape.172) | copy-start | bytes 2654212
  301.7 16.5 %copy-start.7 = (bf16[1536,768]{1,0:T(8,128)(2,1)S(1)}, bf16[1536,768]{1,0:T(8,128)(2,1)}, u32[]{:S(2)}) copy-start(bf16[1536,768]{1,0:T(8,128)(2,1)} %all-reduce.3.cloned.1.call-done) | copy-start | bytes 7077892
  399.5 4.3 %copy-start.4 = (bf16[3084,192]{1,0:T(8,128)(2,1)S(1)}, bf16[3084,192]{1,0:T(8,128)(2,1)}, u32[]{:S(2)}) copy-start(bf16[3084,192]{1,0:T(8,128)(2,1)} %all-reduce.5.cloned.1.call-done) | copy-start | bytes 3552772
Sparse Core Ops, SparseCore 0:
  10.2 22.3 all-gather.2
  39.7 23.2 reduce-scatter.6
  79.2 23.6 reduce-scatter.8
  118.1 23.6 reduce-scatter.10
  164.0 24.8 reduce-scatter.12
  192.9 108.7 all-reduce.2
  306.2 89.2 all-reduce.4

commit v2 on v1

--- a/solution.py
+++ b/solution.py
@@ -1,6 +1,8 @@
 import jax
 import jax.numpy as jnp
 from jax import lax
+from jax.experimental import pallas as pl
+from jax.experimental.pallas import tpu as pltpu
 from jax.sharding import PartitionSpec as P
 
 D = 768
@@ -36,18 +38,209 @@
     return inverse * (scaled - first_mean - normed * second_mean)
 
 
-def sum_rows(partial):
-    return lax.psum_scatter(
-        partial.astype(jnp.bfloat16), "tensor", scatter_dimension=0, tiled=True
-    ).astype(jnp.float32)
-
-
-def all_rows(piece):
-    return lax.all_gather(piece, "tensor", axis=0, tiled=True)
+VMEM = pl.BlockSpec(memory_space=pltpu.VMEM)
+
+
+def greet(peers):
+    barrier = pltpu.get_barrier_semaphore()
+    for peer in peers:
+        pl.semaphore_signal(
+            barrier,
+            inc=1,
+            device_id=(lax.axis_index("dp"), peer),
+            device_id_type=pl.DeviceIdType.MESH,
+        )
+    pl.semaphore_wait(barrier, len(peers))
+
+
+def remote(src, dst, sems, slot, peer):
+    copy = pltpu.make_async_remote_copy(
+        src_ref=src,
+        dst_ref=dst,
+        send_sem=sems[0].at[slot],
+        recv_sem=sems[1].at[slot],
+        device_id=(lax.axis_index("dp"), peer),
+        device_id_type=pl.DeviceIdType.MESH,
+    )
+    copy.start()
+    return copy
+
+
+def call(body, identity, outs, scratch, copies, args):
+    return pl.pallas_call(
+        body,
+        out_shape=outs,
+        in_specs=[VMEM] * len(args),
+        out_specs=[VMEM] * len(outs),
+        scratch_shapes=scratch
+        + [pltpu.SemaphoreType.DMA((copies,)), pltpu.SemaphoreType.DMA((copies,))],
+        compiler_params=pltpu.CompilerParams(
+            collective_id=identity, has_side_effects=True, vmem_limit_bytes=40 << 20
+        ),
+    )(*args)
+
+
+def sum_norm_gather(identity, step, partial, aux, outs):
+    rows, width = partial.shape
+    block = rows // 4
+    count = len(aux)
+
+    def body(*refs):
+        part, ins = refs[0], refs[1 : 1 + count]
+        full, results = refs[1 + count], refs[2 + count : 2 + count + len(outs)]
+        near, held, far = refs[-5:-2]
+        sems = refs[-2:]
+        me = lax.axis_index("tensor")
+        core, chip = me % 2, me // 2
+        mate = chip * 2 + 1 - core
+        across = (1 - chip) * 2 + core
+
+        def at(owner):
+            return pl.ds(pl.multiple_of(owner * block, block), block)
+
+        greet((mate, across))
+        diagonal = (1 - chip) * 2 + 1 - core
+        one = remote(part.at[at(diagonal)], near.at[0], sems, 0, mate)
+        two = remote(part.at[at(mate)], near.at[1], sems, 1, mate)
+        one.wait()
+        held[...] = (
+            part[at(across), :].astype(jnp.float32) + near[0].astype(jnp.float32)
+        ).astype(jnp.bfloat16)
+        three = remote(held, far, sems, 2, across)
+        two.wait()
+        total = part[at(me), :].astype(jnp.float32) + near[1].astype(jnp.float32)
+        three.wait()
+        values = step(total + far[...].astype(jnp.float32), *[ref[...] for ref in ins])
+        full[at(me), :] = values[0].astype(jnp.bfloat16)
+        four = remote(full.at[at(me)], full.at[at(me)], sems, 3, across)
+        five = remote(full.at[at(me)], full.at[at(me)], sems, 4, mate)
+        for ref, value in zip(results, values[1:]):
+            ref[...] = value.astype(ref.dtype)
+        four.wait()
+        six = remote(full.at[at(across)], full.at[at(across)], sems, 5, mate)
+        five.wait()
+        six.wait()
+
+    return call(
+        body,
+        identity,
+        [jax.ShapeDtypeStruct((rows, width), jnp.bfloat16)] + outs,
+        [
+            pltpu.VMEM((2, block, width), jnp.bfloat16),
+            pltpu.VMEM((block, width), jnp.bfloat16),
+            pltpu.VMEM((block, width), jnp.bfloat16),
+        ],
+        6,
+        [partial] + aux,
+    )
+
+
+def gather_inputs(layer_input, cotangent, vectors):
+    rows, width = layer_input.shape
+    block = rows // 4
+
+    def body(x_ref, c_ref, v_ref, x_out, c_out, v_out, *sems):
+        me = lax.axis_index("tensor")
+        peers = [lax.rem(me + d, 4) for d in (1, 2, 3)]
+        greet(peers)
+        copies = []
+        for i, peer in enumerate(peers):
+            copies.append(remote(x_ref, x_out.at[me], sems, 3 * i, peer))
+            copies.append(remote(v_ref, v_out.at[me], sems, 3 * i + 1, peer))
+            src = c_ref.at[pl.ds(pl.multiple_of(peer * block, block), block)]
+            copies.append(remote(src, c_out.at[me], sems, 3 * i + 2, peer))
+        x_out[me] = x_ref[...]
+        v_out[me] = v_ref[...]
+        c_out[me] = c_ref[pl.ds(pl.multiple_of(me * block, block), block), :]
+        for copy in copies:
+            copy.wait()
+
+    return call(
+        body,
+        0,
+        [
+            jax.ShapeDtypeStruct((4, rows, width), layer_input.dtype),
+            jax.ShapeDtypeStruct((4, block, width), cotangent.dtype),
+            jax.ShapeDtypeStruct((4,) + vectors.shape, vectors.dtype),
+        ],
+        [],
+        9,
+        [layer_input, cotangent, vectors],
+    )
+
+
+def scatter_outputs(terms, rows_out):
+    _, rows, width = terms.shape
+    block = rows_out.shape[1]
+
+    def body(t_ref, o_ref, sum_ref, o_out, held, *sems):
+        me = lax.axis_index("tensor")
+        peers = [lax.rem(me + d, 4) for d in (1, 2, 3)]
+        greet(peers)
+        copies = []
+        for i, peer in enumerate(peers):
+            copies.append(remote(t_ref.at[peer], held.at[i], sems, 2 * i, peer))
+        for i, peer in enumerate(peers):
+            copies.append(remote(o_ref.at[peer], o_out.at[me], sems, 2 * i + 1, peer))
+        o_out[me] = o_ref[me]
+        total = t_ref[me].astype(jnp.float32)
+        for i in range(3):
+            copies[i].wait()
+            total = total + held[i].astype(jnp.float32)
+        sum_ref[...] = total
+        for copy in copies[3:]:
+            copy.wait()
+
+    return call(
+        body,
+        1,
+        [
+            jax.ShapeDtypeStruct((rows, width), jnp.float32),
+            jax.ShapeDtypeStruct(rows_out.shape, rows_out.dtype),
+        ],
+        [pltpu.VMEM((3, rows, width), terms.dtype)],
+        6,
+        [terms, rows_out],
+    )
+
+
+def swap(piece, bit):
+    size = lax.axis_size("dp")
+    return lax.ppermute(piece, "dp", [(i, i ^ bit) for i in range(size)])
+
+
+def added(left, right):
+    return (left.astype(jnp.float32) + right.astype(jnp.float32)).astype(jnp.bfloat16)
+
+
+def dp_sum(piece, turn):
+    bits = [1 << i for i in range(lax.axis_size("dp").bit_length() - 1)]
+    bits = bits[turn:] + bits[:turn]
+    me = lax.axis_index("dp")
+    piece = piece.astype(jnp.bfloat16)
+    for bit in bits:
+        upper = (me // bit) % 2 == 1
+        half = piece.shape[0] // 2
+        low, high = piece[:half], piece[half:]
+        other = swap(jnp.where(upper, low, high), bit)
+        piece = added(jnp.where(upper, high, low), other)
+    for bit in reversed(bits):
+        upper = (me // bit) % 2 == 1
+        other = swap(piece, bit)
+        piece = jnp.concatenate(
+            [jnp.where(upper, other, piece), jnp.where(upper, piece, other)], axis=0
+        )
+    return piece.astype(jnp.float32)
+
+
+def dp_sum_small(piece):
+    for i in range(lax.axis_size("dp").bit_length() - 1):
+        piece = piece + swap(piece, 1 << i)
+    return piece
 
 
 def column_sum(rows):
-    return jnp.sum(rows, axis=0)
+    return jnp.sum(rows, axis=0, keepdims=True)
 
 
 def tall_dot(left, right):
@@ -93,26 +286,51 @@
     local_width = triple_weight.shape[2]
     local_heads = local_width // HD
     head_scale = HD ** (-0.5)
-    groups = lax.axis_size("tensor")
     rank = lax.axis_index("tensor")
-    block = tok_count // groups
-    both = lax.all_gather(
-        jnp.concatenate([layer_input, cotangent], axis=0), "tensor", axis=1, tiled=True
-    )
-    gathered = both[:tok_count]
-    own_input = lax.dynamic_slice_in_dim(both, rank * block, block, 0).astype(jnp.float32)
-    upstream = lax.dynamic_slice_in_dim(both, tok_count + rank * block, block, 0).astype(
-        jnp.float32
-    )
-    vectors = lax.all_gather(
-        jnp.stack([output_bias, norm_gain, norm_shift, reduce_bias, final_gain, final_shift]),
-        "tensor",
-        axis=1,
-        tiled=True,
-    )
-    output_bias, norm_gain, norm_shift, reduce_bias, final_gain, final_shift = [
-        vectors[i] for i in range(6)
-    ]
+    block = tok_count // 4
+    stacked = jnp.stack(
+        [output_bias, norm_gain, norm_shift, reduce_bias, final_gain, final_shift] + [final_shift] * 2
+    )
+    x_all, c_all, v_all = gather_inputs(layer_input, cotangent, stacked)
+    gathered = jnp.concatenate([x_all[i] for i in range(4)], axis=1)
+    cot_own = jnp.concatenate([c_all[i] for i in range(4)], axis=1)
+    vectors = jnp.concatenate([v_all[i] for i in range(4)], axis=1)
+    input_own = lax.dynamic_slice_in_dim(gathered, rank * block, block, 0)
+    wide = jax.ShapeDtypeStruct((block, D), jnp.float32)
+    narrow = jax.ShapeDtypeStruct((block, 1), jnp.float32)
+    line = jax.ShapeDtypeStruct((1, D), jnp.float32)
+    half_wide = jax.ShapeDtypeStruct((block, D), jnp.bfloat16)
+
+    def first_step(total, own, vec):
+        hidden = own.astype(jnp.float32) + total + vec[0:1]
+        attended, normed, inverse = norm_forward(hidden, vec[1:2], vec[2:3])
+        return attended, attended, normed, inverse
+
+    def second_step(total, attended, cot, vec):
+        hidden = attended + total + vec[3:4]
+        out, normed, inverse = norm_forward(hidden, vec[4:5], vec[5:6])
+        upstream = cot.astype(jnp.float32)
+        grad = norm_backward(upstream, normed, inverse, vec[4:5])
+        return (
+            grad,
+            grad,
+            out,
+            column_sum(upstream * normed),
+            column_sum(upstream),
+            column_sum(grad),
+        )
+
+    def third_step(total, second_grad, normed, inverse, vec):
+        grad_in = second_grad + total
+        grad = norm_backward(grad_in, normed, inverse, vec[1:2])
+        return (
+            grad,
+            grad,
+            column_sum(grad_in * normed),
+            column_sum(grad_in),
+            column_sum(grad),
+        )
+
     projected = jnp.einsum(
         "td,dcf->tcf", gathered, triple_weight, preferred_element_type=jnp.float32
     )
@@ -135,48 +353,46 @@
         "hqk,khd->qhd", probs_half, value_half, preferred_element_type=jnp.float32
     ).astype(jnp.bfloat16)
     context_flat = context.reshape(tok_count, local_width)
-    first_sum = (
-        own_input
-        + sum_rows(jnp.dot(context_flat, output_weight, preferred_element_type=jnp.float32))
-        + output_bias
-    )
-    attended, normed_one, inv_one = norm_forward(first_sum, norm_gain, norm_shift)
-    attended_half = all_rows(attended.astype(jnp.bfloat16))
+    attended_half, attended, normed_one, inv_one = sum_norm_gather(
+        2,
+        first_step,
+        jnp.dot(context_flat, output_weight, preferred_element_type=jnp.float32).astype(
+            jnp.bfloat16
+        ),
+        [input_own, vectors],
+        [wide, wide, narrow],
+    )
     pre_act = (
         jnp.dot(attended_half, expand_weight, preferred_element_type=jnp.float32) + expand_bias
     )
     activated = gelu_value(pre_act).astype(jnp.bfloat16)
-    second_sum = (
-        attended
-        + sum_rows(jnp.dot(activated, reduce_weight, preferred_element_type=jnp.float32))
-        + reduce_bias
-    )
-    out_f, normed_two, inv_two = norm_forward(second_sum, final_gain, final_shift)
-    layer_output = lax.all_to_all(
-        out_f.astype(jnp.bfloat16), "tensor", split_axis=1, concat_axis=0, tiled=True
-    )
-    final_gain_grad = column_sum(upstream * normed_two)
-    final_shift_grad = column_sum(upstream)
-    second_grad = norm_backward(upstream, normed_two, inv_two, final_gain)
-    second_half = all_rows(second_grad.astype(jnp.bfloat16))
+    second_half, second_grad, out_rows, final_gain_grad, final_shift_grad, reduce_bias_grad = (
+        sum_norm_gather(
+            3,
+            second_step,
+            jnp.dot(activated, reduce_weight, preferred_element_type=jnp.float32).astype(
+                jnp.bfloat16
+            ),
+            [attended, cot_own, vectors],
+            [wide, half_wide, line, line, line],
+        )
+    )
     reduce_weight_grad = tall_dot(activated, second_half)
-    reduce_bias_grad = column_sum(second_grad)
     act_grad = wide_dot(second_half, reduce_weight) * gelu_slope(pre_act)
     act_half = act_grad.astype(jnp.bfloat16)
     expand_weight_grad = tall_dot(attended_half, act_half)
-    expand_bias_grad = column_sum(act_grad)
-    feed_sum = lax.psum(
-        jnp.concatenate([reduce_weight_grad, expand_weight_grad], axis=0).astype(jnp.bfloat16),
-        "dp",
-    )
-    split = reduce_weight_grad.shape[0]
-    attended_grad = second_grad + sum_rows(wide_dot(act_half, expand_weight))
-    norm_gain_grad = column_sum(attended_grad * normed_one)
-    norm_shift_grad = column_sum(attended_grad)
-    first_grad = norm_backward(attended_grad, normed_one, inv_one, norm_gain)
-    first_half = all_rows(first_grad.astype(jnp.bfloat16))
+    expand_bias_grad = jnp.sum(act_grad, axis=0)
+    reduce_weight_grad = dp_sum(reduce_weight_grad, 0)
+    expand_weight_grad = dp_sum(expand_weight_grad, 1)
+    first_half, first_grad, norm_gain_grad, norm_shift_grad, output_bias_grad = sum_norm_gather(
+        4,
+        third_step,
+        wide_dot(act_half, expand_weight).astype(jnp.bfloat16),
+        [second_grad, normed_one, inv_one, vectors],
+        [wide, line, line, line],
+    )
     output_weight_grad = tall_dot(context_flat, first_half)
-    output_bias_grad = column_sum(first_grad)
+    output_weight_grad = dp_sum(output_weight_grad, 0)
     grad_part = (
         wide_dot(first_half, output_weight)
         .astype(jnp.bfloat16)
@@ -205,10 +421,14 @@
     triple_grad = jnp.einsum(
         "td,tcf->dcf", gathered, triple_half, preferred_element_type=jnp.float32
     )
+    flat = triple_grad.reshape(D, -1)
+    triple_grad = jnp.concatenate(
+        [dp_sum(flat[: D // 2], 0), dp_sum(flat[D // 2 :], 1)], axis=0
+    ).reshape(triple_grad.shape)
     input_terms = jnp.einsum(
         "tcf,dcf->td", triple_half, triple_weight, preferred_element_type=jnp.float32
     )
-    smalls = jnp.stack(
+    smalls = jnp.concatenate(
         [
             output_bias_grad,
             norm_gain_grad,
@@ -216,36 +436,32 @@
             reduce_bias_grad,
             final_gain_grad,
             final_shift_grad,
-        ]
+            jnp.zeros((10, D), jnp.float32),
+        ],
+        axis=0,
     )
     own_rows = lax.dynamic_slice_in_dim(input_terms, rank * block, block, 0) + first_grad
     input_terms = lax.dynamic_update_slice_in_dim(input_terms, own_rows, rank * block, 0)
-    shares = lax.psum_scatter(
-        jnp.concatenate([input_terms, smalls, jnp.zeros((10, D), jnp.float32)], axis=0).astype(jnp.bfloat16),
-        "tensor",
-        scatter_dimension=1,
-        tiled=True,
-    ).astype(jnp.float32)
+    terms = jnp.concatenate([input_terms, smalls], axis=0).astype(jnp.bfloat16)
+    shares, layer_output = scatter_outputs(
+        jnp.stack(jnp.split(terms, 4, axis=1)), jnp.stack(jnp.split(out_rows, 4, axis=1))
+    )
+    layer_output = layer_output.reshape(tok_count, local_width)
     input_grad = shares[:tok_count]
-    pieces = [
-        triple_grad,
-        output_weight_grad,
-        expand_bias_grad,
-        jnp.sum(query_grad, axis=0),
-        jnp.sum(value_grad, axis=0),
-        shares[tok_count : tok_count + 6],
-    ]
-    packed = jnp.concatenate([p.reshape(-1, local_width) for p in pieces], axis=0)
-    packed, feed_sum = lax.optimization_barrier((packed.astype(jnp.bfloat16), feed_sum))
-    packed = lax.psum(packed, "dp").astype(jnp.float32)
-    reduce_weight_grad = feed_sum[:split].astype(jnp.float32)
-    expand_weight_grad = feed_sum[split:].astype(jnp.float32)
-    outs, at = [], 0
-    for p in pieces:
-        count = p.size // local_width
-        outs.append(packed[at : at + count].reshape(p.shape))
-        at += count
-    triple_grad, output_weight_grad, expand_bias_grad, query_sum, value_sum, small_sums = outs
+    packed = jnp.concatenate(
+        [
+            expand_bias_grad.reshape(-1, local_width),
+            jnp.sum(query_grad, axis=0, keepdims=True),
+            jnp.sum(value_grad, axis=0, keepdims=True),
+            shares[tok_count : tok_count + 6],
+        ],
+        axis=0,
+    )
+    packed = dp_sum_small(packed)
+    extra = packed.shape[0] - 8
+    expand_bias_grad = packed[:extra].reshape(-1)
+    query_sum, value_sum = packed[extra], packed[extra + 1]
+    small_sums = packed[extra + 2 :]
     return (
         layer_output,
         input_grad,

time: 415 us -> 264 us (0.64)
  waiting for transfers between devices: 275 us -> 81.9 us
  Pallas kernels: 0 us -> 83.1 us
  blocking collectives: 38.8 us -> 0 us
  starting transfers between devices: 0.29 us -> 36.7 us
  local copies, waits for them, and re-layouts: 41.6 us -> 14.4 us
  between operations: 14.7 us -> 1.69 us
  other arithmetic: 20.5 us -> 25.9 us
    psum x2 -> x0, waiting for transfers between devices: 180 us -> none  [the longest x1 105 us: per_device(): lax.psum(jnp.concatenate([reduce_weight_grad, expand_weight_grad], axis=0...]
    pallas_call x0 -> x5, Pallas kernels: none -> 83.1 us  [call(): pl.pallas_call(body, out_shape=outs, in_specs=[VMEM] * len(args), out_spe...]
    ppermute x0 -> x33, waiting for transfers between devices: none -> 81.9 us  [swap(): return lax.ppermute(piece, 'dp', [(i, i ^ bit) for i in range(size)])]
    reduce_scatter x3 -> x0, waiting for transfers between devices: 63.9 us -> none  [sum_rows(): lax.psum_scatter(partial.astype(jnp.bfloat16), 'tensor', scatter_dimensio...]
    ppermute x0 -> x33, starting transfers between devices: none -> 36.7 us  [swap(): return lax.ppermute(piece, 'dp', [(i, i ^ bit) for i in range(size)])]
    all_gather x4 -> x0, blocking collectives: 30.1 us -> none  [the longest x3 24.9 us: all_rows(): return lax.all_gather(piece, 'tensor', axis=0, tiled=True)]
    all_gather x1 -> x0, waiting for transfers between devices: 21.4 us -> none  [per_device(): lax.all_gather(jnp.concatenate([layer_input, cotangent], axis=0), 'tensor...]
    unnamed x8 -> x0, waiting for transfers between devices: 10.1 us -> none
  transfers between devices with their start and end apart: 7 -> 33, of which waited for: 7 -> 21; matrix products, arithmetic and copies ran while one was open for 9% -> 16% of each run, Pallas kernels for 0% -> 6%
where the time goes in v2:
time: 264 us; the launch traced here: 263 us
  Pallas kernels  83.1 us (31%)
  waiting for transfers between devices  81.9 us (31%)
  starting transfers between devices  36.7 us (14%)
  other arithmetic  25.9 us (10%)
  matrix products  19.4 us (7%)
  local copies, waits for them, and re-layouts  14.4 us (5%)
    pallas_call x5, Pallas kernels, call(): pl.pallas_call(body, out_shape=outs, in_specs=[VMEM] * len(args), out_spe...  83.1 us
    ppermute x33, waiting for transfers between devices, swap(): return lax.ppermute(piece, 'dp', [(i, i ^ bit) for i in range(size)])  81.9 us
    ppermute x33, starting transfers between devices, swap(): return lax.ppermute(piece, 'dp', [(i, i ^ bit) for i in range(size)])  36.7 us
    unnamed x68, local copies, waits for them, and re-layouts  6.85 us
    convert_element_type x15, other arithmetic, added(): (left.astype(jnp.float32) + right.astype(jnp.float32)).astype(jnp.bfloat16)  5.66 us
  transfers between devices with their start and end apart: 33, of which 21 were waited for; matrix products, arithmetic and copies ran while one was open for 16% of the time, Pallas kernels for 6%

profile of v2, /device:TPU:0, one launch (start us, length us, event | category | flops | bytes accessed | tf_op | source)
XLA Modules:
  0.0 263.1 jit_solution(12959018462876131521)
XLA Ops:
  3.8 18.1 %shard_map.254 = (bf16[4,512,192]{2,1,0:T(8,128)(2,1)S(1)}, bf16[4,128,192]{2,1,0:T(8,128)(2,1)S(1)}, f32[4,8,192]{2,1,0:T(8,128)S(1)}) custom-call(bf16[512,192]{1,0:T(8,128)(2,1)S(1)} %copy.29.x_ref, bf16[512,192]{1,0:T(8,128)(2,1)S(1)} %copy.30.c_ref, f32[8,192]{1,0:T(8,128)S(1)} %stack.66.v_ref), custom_call_target="tpu_custom_call" | custom-call | tf_op jit(solution)/shard_map/pallas_call | solution.py:70
  28.7 16.4 %shard_map.255 = (bf16[512,768]{1,0:T(8,128)(2,1)S(1)}, f32[128,768]{1,0:T(8,128)S(1)}, f32[128,768]{1,0:T(8,128)S(1)}, f32[128,1]{1,0:T(8,128)S(1)}) custom-call(bf16[512,768]{1,0:T(8,128)(2,1)S(1)} %convolution_convert_fusion.4.refs_0_, bf16[128,768]{1,0:T(8,128)(2,1)S(1)} %constant_dynamic-slice_fusion.refs_1_, ...), custom_call_target="tpu_custom_call" | custom-call | tf_op jit(solution)/shard_map/pallas_call | solution.py:70
  47.3 15.9 %shard_map.256 = (bf16[512,768]{1,0:T(8,128)(2,1)S(1)}, f32[128,768]{1,0:T(8,128)S(1)}, bf16[128,768]{1,0:T(8,128)(2,1)S(1)}, f32[1,768]{1,0:T(1,128)S(1)}, f32[1,768]{1,0:T(1,128)S(1)}, /*index=5*/f32[1,768]{1,0:T(1,128)S(1)}) custom-call(bf16[512,768]{1,0:T(8,128)(2,1)S(1)} %convolution_convert_fusion.3.refs_0_, f32[128,768]{1,0:T(8,128)S(1)} %get-tuple-element.37.refs_1_, ...), custom_call_target="tpu_custom_call" | custom-call | tf_op jit(solution)/shard_map/pallas_call | solution.py:70
  65.2 16.1 %shard_map.257 = (bf16[512,768]{1,0:T(8,128)(2,1)S(1)}, f32[128,768]{1,0:T(8,128)S(1)}, f32[1,768]{1,0:T(1,128)S(1)}, f32[1,768]{1,0:T(1,128)S(1)}, f32[1,768]{1,0:T(1,128)S(1)}) custom-call(bf16[512,768]{1,0:T(8,128)(2,1)S(1)} %convolution_convert_fusion.2.refs_0_, f32[128,768]{1,0:T(8,128)S(1)} %get-tuple-element.40.refs_1_, ...), custom_call_target="tpu_custom_call" | custom-call | tf_op jit(solution)/shard_map/pallas_call | solution.py:70
  83.1 1.5 collective-permute-start.15
  84.6 1.4 convolution_convert_fusion.8
  87.0 3.7 %fusion.18 = (f32[3,64]{1,0:T(4,128)S(1)}, bf16[512,3,64]{0,2,1:T(8,128)(2,1)}) fusion(bf16[512,3,64]{0,2,1:T(8,128)(2,1)S(1)} %bitcast.143, f32[3,512,512]{1,2,0:T(8,128)} %copy-done.2, f32[3,512]{1,0:T(4,128)S(1)} %log_add_fusion, pred[512,512]{0,1:T(8,128)(4,1)S(1)} %copy-done.11), kind=kOutput, calls=%fused_computation.149 | convolution fusion | flops 104005440 | bytes 3808000 | tf_op jit(solution)/shard_map/hqk,qhd->khd/dot_general | solution.py:404
  90.7 1.4 multiply_convert_fusion
  92.1 1.3 convolution_convert_fusion.6
  97.3 1.6 collective-permute-start.6
  99.4 2.0 convolution_bitcast_fusion
  101.8 1.8 add_dynamic-update-slice_fusion
  103.6 2.4 convert.50
  106.0 3.0 %concatenate.78 = bf16[528,768]{1,0:T(8,128)(2,1)S(1)} concatenate(bf16[512,768]{1,0:T(8,128)(2,1)} %convert.50, bf16[1,768]{1,0:T(2,128)(2,1)S(1)} %convert.51, bf16[1,768]{1,0:T(2,128)(2,1)S(1)} %convert.52, bf16[1,768]{1,0:T(2,128)(2,1)S(1)} %convert.53, bf16[1,768]{1,0:T(2,128)(2,1)S(1)} %convert.54, bf16[1,768]{1,0:T(2,128)(2,1)S(1)} %convert.55, ...), dimensions={0} | concatenate | bytes 1622016 | tf_op jit(solution)/shard_map/concatenate | solution.py:445
  109.6 16.6 %shard_map.258 = (f32[528,192]{1,0:T(8,128)S(1)}, bf16[4,128,192]{2,1,0:T(8,128)(2,1)S(1)}) custom-call(bf16[4,528,192]{2,1,0:T(8,128)(2,1)S(1)} %pad_maximum_fusion.t_ref, bf16[4,128,192]{2,1,0:T(8,128)(2,1)S(1)} %pad_maximum_fusion.9.o_ref), custom_call_target="tpu_custom_call" | custom-call | tf_op jit(solution)/shard_map/pallas_call | solution.py:70
  126.3 1.6 collective-permute-start.12
  130.1 1.6 collective-permute-start.13
  132.5 13.3 %collective-permute-done.13 = f32[12,192]{1,0:T(8,128)S(1)} collective-permute-done((f32[12,192]{1,0:T(8,128)S(1)}, f32[12,192]{1,0:T(8,128)S(1)}, u32[]{:S(2)}, u32[]{:S(2)}) %collective-permute-start.13) | collective-permute-done | bytes 9248 | tf_op jit(solution)/shard_map/ppermute | solution.py:209
  145.9 2.6 collective-permute-start.14
  154.1 2.1 collective-permute-done.16
  156.2 2.0 collective-permute-start.17
  161.5 1.6 collective-permute-done.17
  163.8 2.9 %collective-permute-start.1 = (bf16[96,576]{0,1:T(8,128)(2,1)S(1)}, bf16[96,576]{0,1:T(8,128)(2,1)S(1)}, u32[]{:S(2)}, u32[]{:S(2)}) collective-permute-start(bf16[96,576]{0,1:T(8,128)(2,1)S(1)} %broadcast_select_fusion.40), channel_id=1, source_target_pairs={{0,8},{4,12},{8,0},{12,4},{16,24},{20,28},{24,16},{28,20},{1,9},{5... | collective-permute-start | bytes 331784 | tf_op jit(solution)/shard_map/ppermute | solution.py:209
  166.7 1.8 collective-permute-done.18
  168.9 1.5 collective-permute-start.8
  171.1 2.5 collective-permute-start.2
  173.7 1.5 collective-permute-start.20
  176.4 2.9 %collective-permute-done.2 = bf16[48,576]{0,1:T(8,128)(2,1)S(1)} collective-permute-done((bf16[48,576]{0,1:T(8,128)(2,1)S(1)}, bf16[48,576]{0,1:T(8,128)(2,1)S(1)}, u32[]{:S(2)}, u32[]{:S(2)}) %collective-permute-start.2) | collective-permute-done | bytes 55328 | tf_op jit(solution)/shard_map/ppermute | solution.py:209
  181.0 3.1 %collective-permute-start.10 = (bf16[96,576]{0,1:T(8,128)(2,1)S(1)}, bf16[96,576]{0,1:T(8,128)(2,1)S(1)}, u32[]{:S(2)}, u32[]{:S(2)}) collective-permute-start(bf16[96,576]{0,1:T(8,128)(2,1)S(1)} %pad_maximum_fusion.12), channel_id=1, source_target_pairs={{0,16},{4,20},{8,24},{12,28},{16,0},{20,4},{24,8},{28,12},{1,17},{... | collective-permute-start | bytes 331784 | tf_op jit(solution)/shard_map/ppermute | solution.py:209
  184.1 6.8 %collective-permute-done.3 = bf16[48,576]{0,1:T(8,128)(2,1)S(1)} collective-permute-done((bf16[48,576]{0,1:T(8,128)(2,1)S(1)}, bf16[48,576]{0,1:T(8,128)(2,1)S(1)}, u32[]{:S(2)}, u32[]{:S(2)}) %collective-permute-start.3) | collective-permute-done | bytes 55328 | tf_op jit(solution)/shard_map/ppermute | solution.py:209
  192.9 1.6 collective-permute-start.11
  194.5 3.4 %collective-permute-done.4 = bf16[96,576]{0,1:T(8,128)(2,1)S(1)} collective-permute-done((bf16[96,576]{0,1:T(8,128)(2,1)S(1)}, bf16[96,576]{0,1:T(8,128)(2,1)S(1)}, u32[]{:S(2)}, u32[]{:S(2)}) %collective-permute-start.4) | collective-permute-done | bytes 110624 | tf_op jit(solution)/shard_map/ppermute | solution.py:209
  198.7 1.3 add_convert_fusion
  200.2 1.3 add_convert_fusion.1
  201.5 2.3 collective-permute-start.22
  203.8 5.0 %collective-permute-done.11 = bf16[192,576]{0,1:T(8,128)(2,1)S(1)} collective-permute-done((bf16[192,576]{0,1:T(8,128)(2,1)S(1)}, bf16[192,576]{0,1:T(8,128)(2,1)S(1)}, u32[]{:S(2)}, u32[]{:S(2)}) %collective-permute-start.11) | collective-permute-done | bytes 221216 | tf_op jit(solution)/shard_map/ppermute | solution.py:209
  209.1 4.2 %collective-permute-done.28 = bf16[192,768]{1,0:T(8,128)(2,1)S(1)} collective-permute-done((bf16[192,768]{1,0:T(8,128)(2,1)S(1)}, bf16[192,768]{1,0:T(8,128)(2,1)S(1)}, u32[]{:S(2)}, u32[]{:S(2)}) %collective-permute-start.28) | collective-permute-done | bytes 294944 | tf_op jit(solution)/shard_map/ppermute | solution.py:209
  213.5 5.3 %collective-permute-done.22 = bf16[192,768]{1,0:T(8,128)(2,1)S(1)} collective-permute-done((bf16[192,768]{1,0:T(8,128)(2,1)S(1)}, bf16[192,768]{1,0:T(8,128)(2,1)S(1)}, u32[]{:S(2)}, u32[]{:S(2)}) %collective-permute-start.22) | collective-permute-done | bytes 294944 | tf_op jit(solution)/shard_map/ppermute | solution.py:209
  219.6 1.6 collective-permute-done.29
  221.4 3.5 %collective-permute-done.23 = bf16[96,768]{1,0:T(8,128)(2,1)S(1)} collective-permute-done((bf16[96,768]{1,0:T(8,128)(2,1)S(1)}, bf16[96,768]{1,0:T(8,128)(2,1)S(1)}, u32[]{:S(2)}, u32[]{:S(2)}) %collective-permute-start.23) | collective-permute-done | bytes 147488 | tf_op jit(solution)/shard_map/ppermute | solution.py:209
  226.0 4.1 %collective-permute-done.30 = bf16[96,768]{1,0:T(8,128)(2,1)S(1)} collective-permute-done((bf16[96,768]{1,0:T(8,128)(2,1)S(1)}, bf16[96,768]{1,0:T(8,128)(2,1)S(1)}, u32[]{:S(2)}, u32[]{:S(2)}) %collective-permute-start.30) | collective-permute-done | bytes 147488 | tf_op jit(solution)/shard_map/ppermute | solution.py:209
  230.3 2.3 collective-permute-start.25
  232.6 11.8 %collective-permute-done.31 = bf16[192,768]{1,0:T(8,128)(2,1)S(1)} collective-permute-done((bf16[192,768]{1,0:T(8,128)(2,1)S(1)}, bf16[192,768]{1,0:T(8,128)(2,1)S(1)}, u32[]{:S(2)}, u32[]{:S(2)}) %collective-permute-start.31) | collective-permute-done | bytes 294944 | tf_op jit(solution)/shard_map/ppermute | solution.py:209
  244.9 1.6 collective-permute-done.25
  246.8 1.5 maximum_convert_fusion.2
  248.3 10.7 %collective-permute-done.32 = bf16[384,768]{1,0:T(8,128)(2,1)S(1)} collective-permute-done((bf16[384,768]{1,0:T(8,128)(2,1)S(1)}, bf16[384,768]{1,0:T(8,128)(2,1)S(1)}, u32[]{:S(2)}, u32[]{:S(2)}) %collective-permute-start.32) | collective-permute-done | bytes 589856 | tf_op jit(solution)/shard_map/ppermute | solution.py:209
  259.2 1.6 maximum_convert_fusion.1
  261.4 1.6 maximum_convert_fusion
  (213 shorter events, 45.7 us)
Async XLA Ops:
  0.6 44.4 %copy-start = (bf16[768,768]{1,0:T(8,128)(2,1)S(1)}, bf16[768,768]{1,0:T(8,128)(2,1)}, u32[]{:S(2)}) copy-start(bf16[768,768]{1,0:T(8,128)(2,1)} %param.23) | copy-start | bytes 3538948
  22.3 2.7 %copy-start.4 = (bf16[512,768]{1,0:T(8,128)(2,1)}, bf16[512,768]{1,0:T(8,128)(2,1)S(1)}, u32[]{:S(2)}) copy-start(bf16[512,768]{1,0:T(8,128)(2,1)S(1)} %pad_maximum_fusion.1) | copy-start | bytes 2359300
  25.9 2.7 %copy-start.2 = (f32[3,512,512]{1,2,0:T(8,128)}, f32[3,512,512]{1,2,0:T(8,128)S(1)}, u32[]{:S(2)}) copy-start(f32[3,512,512]{1,2,0:T(8,128)S(1)} %get-tuple-element.137) | copy-start | bytes 9437188
  28.2 53.1 %copy-start.14 = (bf16[3,64,512]{2,1,0:T(8,128)(2,1)}, bf16[3,64,512]{2,1,0:T(8,128)(2,1)S(1)}, u32[]{:S(2)}) copy-start(bf16[3,64,512]{2,1,0:T(8,128)(2,1)S(1)} %convolution_convert_fusion.7) | copy-start | bytes 589828
  28.2 16.9 %copy-start.27 = (f32[768]{0:T(1024)S(1)}, f32[768]{0:T(1024)}, u32[]{:S(2)}) copy-start(f32[768]{0:T(1024)} %param.24) | copy-start | bytes 9220
  83.1 68.6 %collective-permute-start.15 = (bf16[96,768]{1,0:T(8,128)(2,1)}, bf16[96,768]{1,0:T(8,128)(2,1)S(1)}, u32[]{:S(2)}, u32[]{:S(2)}) collective-permute-start(bf16[96,768]{1,0:T(8,128)(2,1)} %broadcast_select_fusion.28), channel_id=1, source_target_pairs={{0,4},{4,0},{8,12},{12,8},{16,20},{20,16},{24,28},{28,24},{1,5},{5... | collective-permute-start | bytes 442376 | tf_op jit(solution)/shard_map/ppermute | solution.py:209
  84.6 2.4 copy-start.11
  87.0 3.7 %copy-start.3 = (f32[3,512,512]{1,2,0:T(8,128)S(1)}, f32[3,512,512]{1,2,0:T(8,128)}, u32[]{:S(2)}) copy-start(f32[3,512,512]{1,2,0:T(8,128)} %copy-done.2) | copy-start | bytes 9437188
  87.0 3.7 %copy-start.22 = (f32[512,1,192]{0,2,1:T(8,128)S(1)}, f32[512,1,192]{0,2,1:T(8,128)}, u32[]{:S(2)}) copy-start(f32[512,1,192]{0,2,1:T(8,128)} %get-tuple-element.75) | copy-start | bytes 1179652
  96.1 3.4 %copy-start.19 = (bf16[768,3,192]{0,2,1:T(8,128)(2,1)S(1)}, bf16[768,3,192]{0,2,1:T(8,128)(2,1)}, u32[]{:S(2)}) copy-start(bf16[768,3,192]{0,2,1:T(8,128)(2,1)} %param.17) | copy-start | bytes 2654212
  96.1 3.4 %copy-start.23 = (bf16[512,3,64]{0,2,1:T(8,128)(2,1)S(1)}, bf16[512,3,64]{0,2,1:T(8,128)(2,1)}, u32[]{:S(2)}) copy-start(bf16[512,3,64]{0,2,1:T(8,128)(2,1)} %get-tuple-element.99) | copy-start | bytes 589828
  97.3 60.9 %collective-permute-start.6 = (bf16[192,576]{0,1:T(8,128)(2,1)}, bf16[192,576]{0,1:T(8,128)(2,1)}, u32[]{:S(2)}, u32[]{:S(2)}) collective-permute-start(bf16[192,576]{0,1:T(8,128)(2,1)} %bitcast.54), channel_id=1, source_target_pairs={{0,8},{4,12},{8,0},{12,4},{16,24},{20,28},{24,16},{28,20},{1,9},{5... | collective-permute-start | bytes 663560 | tf_op jit(solution)/shard_map/ppermute | solution.py:209
  98.9 61.6 %collective-permute-start = (bf16[192,576]{0,1:T(8,128)(2,1)}, bf16[192,576]{0,1:T(8,128)(2,1)}, u32[]{:S(2)}, u32[]{:S(2)}) collective-permute-start(bf16[192,576]{0,1:T(8,128)(2,1)} %bitcast.50), channel_id=1, source_target_pairs={{0,4},{4,0},{8,12},{12,8},{16,20},{20,16},{24,28},{28,24},{1,5},{5... | collective-permute-start | bytes 663560 | tf_op jit(solution)/shard_map/ppermute | solution.py:209
  109.4 18.5 %copy-start.31 = (bf16[512,768]{1,0:T(8,128)(2,1)S(1)}, bf16[512,768]{1,0:T(8,128)(2,1)}, u32[]{:S(2)}) copy-start(bf16[512,768]{1,0:T(8,128)(2,1)} %copy-done.30) | copy-start | bytes 2359300
  126.3 3.8 %collective-permute-start.12 = (f32[12,192]{1,0:T(8,128)S(1)}, f32[12,192]{1,0:T(8,128)S(1)}, u32[]{:S(2)}, u32[]{:S(2)}) collective-permute-start(f32[12,192]{1,0:T(8,128)S(1)} %pad_maximum_fusion.16), channel_id=1, source_target_pairs={{0,4},{4,0},{8,12},{12,8},{16,20},{20,16},{24,28},{28,24},{1,5},{5... | collective-permute-start | bytes 27656 | tf_op jit(solution)/shard_map/ppermute | solution.py:209
  128.7 3.8 %copy-start.6 = (bf16[768,768]{1,0:T(8,128)(2,1)}, bf16[768,768]{1,0:T(8,128)(2,1)S(1)}, u32[]{:S(2)}) copy-start(bf16[768,768]{1,0:T(8,128)(2,1)S(1)} %convolution_convert_fusion.1) | copy-start | bytes 3538948
  128.7 3.0 %copy-start.29 = (bf16[512,768]{1,0:T(8,128)(2,1)S(1)}, bf16[512,768]{1,0:T(8,128)(2,1)}, u32[]{:S(2)}) copy-start(bf16[512,768]{1,0:T(8,128)(2,1)} %copy-done.28) | copy-start | bytes 2359300
  129.6 70.6 %collective-permute-start.21 = (bf16[384,768]{1,0:T(8,128)(2,1)}, bf16[384,768]{1,0:T(8,128)(2,1)}, u32[]{:S(2)}, u32[]{:S(2)}) collective-permute-start(bf16[384,768]{1,0:T(8,128)(2,1)} %broadcast_select_fusion.5), channel_id=1, source_target_pairs={{0,8},{4,12},{8,0},{12,4},{16,24},{20,28},{24,16},{28,20},{1,9},{5... | collective-permute-start | bytes 1769480 | tf_op jit(solution)/shard_map/ppermute | solution.py:209
  130.1 15.7 %collective-permute-start.13 = (f32[12,192]{1,0:T(8,128)S(1)}, f32[12,192]{1,0:T(8,128)S(1)}, u32[]{:S(2)}, u32[]{:S(2)}) collective-permute-start(f32[12,192]{1,0:T(8,128)S(1)} %fusion.13), channel_id=1, source_target_pairs={{0,8},{4,12},{8,0},{12,4},{16,24},{20,28},{24,16},{28,20},{1,9},{5... | collective-permute-start | bytes 27656 | tf_op jit(solution)/shard_map/ppermute | solution.py:209
  145.9 5.3 %collective-permute-start.14 = (f32[12,192]{1,0:T(8,128)S(1)}, f32[12,192]{1,0:T(8,128)S(1)}, u32[]{:S(2)}, u32[]{:S(2)}) collective-permute-start(f32[12,192]{1,0:T(8,128)S(1)} %add.170), channel_id=1, source_target_pairs={{0,16},{4,20},{8,24},{12,28},{16,0},{20,4},{24,8},{28,12},{1,17},{... | collective-permute-start | bytes 27656 | tf_op jit(solution)/shard_map/ppermute | solution.py:209
  149.4 8.9 %copy-start.17 = (bf16[192,3,192]{0,2,1:T(8,128)(2,1)S(1)}, bf16[192,3,192]{0,2,1:T(8,128)(2,1)}, u32[]{:S(2)}) copy-start(bf16[192,3,192]{0,2,1:T(8,128)(2,1)} %get-tuple-element.81) | copy-start | bytes 663556
  150.2 10.3 %copy-start.16 = (bf16[192,3,192]{0,2,1:T(8,128)(2,1)S(1)}, bf16[192,3,192]{0,2,1:T(8,128)(2,1)}, u32[]{:S(2)}) copy-start(bf16[192,3,192]{0,2,1:T(8,128)(2,1)} %get-tuple-element.80) | copy-start | bytes 663556
  151.1 47.6 %collective-permute-start.27 = (bf16[384,768]{1,0:T(8,128)(2,1)}, bf16[384,768]{1,0:T(8,128)(2,1)}, u32[]{:S(2)}, u32[]{:S(2)}) collective-permute-start(bf16[384,768]{1,0:T(8,128)(2,1)} %broadcast_select_fusion.2), channel_id=1, source_target_pairs={{0,4},{4,0},{8,12},{12,8},{16,20},{20,16},{24,28},{28,24},{1,5},{5... | collective-permute-start | bytes 1769480 | tf_op jit(solution)/shard_map/ppermute | solution.py:209
  151.8 4.4 %collective-permute-start.16 = (bf16[48,768]{1,0:T(8,128)(2,1)S(1)}, bf16[48,768]{1,0:T(8,128)(2,1)S(1)}, u32[]{:S(2)}, u32[]{:S(2)}) collective-permute-start(bf16[48,768]{1,0:T(8,128)(2,1)S(1)} %broadcast_select_fusion.43), channel_id=1, source_target_pairs={{0,8},{4,12},{8,0},{12,4},{16,24},{20,28},{24,16},{28,20},{1,9},{5... | collective-permute-start | bytes 221192 | tf_op jit(solution)/shard_map/ppermute | solution.py:209
  156.2 6.9 %collective-permute-start.17 = (bf16[24,768]{1,0:T(8,128)(2,1)S(1)}, bf16[24,768]{1,0:T(8,128)(2,1)S(1)}, u32[]{:S(2)}, u32[]{:S(2)}) collective-permute-start(bf16[24,768]{1,0:T(8,128)(2,1)S(1)} %broadcast_select_fusion.46), channel_id=1, source_target_pairs={{0,16},{4,20},{8,24},{12,28},{16,0},{20,4},{24,8},{28,12},{1,17},{... | collective-permute-start | bytes 110600 | tf_op jit(solution)/shard_map/ppermute | solution.py:209
  159.4 9.2 %collective-permute-start.7 = (bf16[96,576]{0,1:T(8,128)(2,1)S(1)}, bf16[96,576]{0,1:T(8,128)(2,1)S(1)}, u32[]{:S(2)}, u32[]{:S(2)}) collective-permute-start(bf16[96,576]{0,1:T(8,128)(2,1)S(1)} %broadcast_select_fusion.34), channel_id=1, source_target_pairs={{0,16},{4,20},{8,24},{12,28},{16,0},{20,4},{24,8},{28,12},{1,17},{... | collective-permute-start | bytes 331784 | tf_op jit(solution)/shard_map/ppermute | solution.py:209
  163.2 5.4 %collective-permute-start.18 = (bf16[24,768]{1,0:T(8,128)(2,1)S(1)}, bf16[24,768]{1,0:T(8,128)(2,1)S(1)}, u32[]{:S(2)}, u32[]{:S(2)}) collective-permute-start(bf16[24,768]{1,0:T(8,128)(2,1)S(1)} %add_convert_fusion.18), channel_id=1, source_target_pairs={{0,16},{4,20},{8,24},{12,28},{16,0},{20,4},{24,8},{28,12},{1,17},{... | collective-permute-start | bytes 110600 | tf_op jit(solution)/shard_map/ppermute | solution.py:209
  163.8 7.1 %collective-permute-start.1 = (bf16[96,576]{0,1:T(8,128)(2,1)S(1)}, bf16[96,576]{0,1:T(8,128)(2,1)S(1)}, u32[]{:S(2)}, u32[]{:S(2)}) collective-permute-start(bf16[96,576]{0,1:T(8,128)(2,1)S(1)} %broadcast_select_fusion.40), channel_id=1, source_target_pairs={{0,8},{4,12},{8,0},{12,4},{16,24},{20,28},{24,16},{28,20},{1,9},{5... | collective-permute-start | bytes 331784 | tf_op jit(solution)/shard_map/ppermute | solution.py:209
  168.5 5.1 %collective-permute-start.19 = (bf16[48,768]{1,0:T(8,128)(2,1)S(1)}, bf16[48,768]{1,0:T(8,128)(2,1)S(1)}, u32[]{:S(2)}, u32[]{:S(2)}) collective-permute-start(bf16[48,768]{1,0:T(8,128)(2,1)S(1)} %pad_maximum_fusion.14), channel_id=1, source_target_pairs={{0,8},{4,12},{8,0},{12,4},{16,24},{20,28},{24,16},{28,20},{1,9},{5... | collective-permute-start | bytes 221192 | tf_op jit(solution)/shard_map/ppermute | solution.py:209
  168.9 6.2 %collective-permute-start.8 = (bf16[48,576]{0,1:T(8,128)(2,1)S(1)}, bf16[48,576]{0,1:T(8,128)(2,1)S(1)}, u32[]{:S(2)}, u32[]{:S(2)}) collective-permute-start(bf16[48,576]{0,1:T(8,128)(2,1)S(1)} %broadcast_select_fusion.31), channel_id=1, source_target_pairs={{0,4},{4,0},{8,12},{12,8},{16,20},{20,16},{24,28},{28,24},{1,5},{5... | collective-permute-start | bytes 165896 | tf_op jit(solution)/shard_map/ppermute | solution.py:209
  171.1 8.2 %collective-permute-start.2 = (bf16[48,576]{0,1:T(8,128)(2,1)S(1)}, bf16[48,576]{0,1:T(8,128)(2,1)S(1)}, u32[]{:S(2)}, u32[]{:S(2)}) collective-permute-start(bf16[48,576]{0,1:T(8,128)(2,1)S(1)} %broadcast_select_fusion.37), channel_id=1, source_target_pairs={{0,16},{4,20},{8,24},{12,28},{16,0},{20,4},{24,8},{28,12},{1,17},{... | collective-permute-start | bytes 165896 | tf_op jit(solution)/shard_map/ppermute | solution.py:209
  173.7 17.5 %collective-permute-start.20 = (bf16[96,768]{1,0:T(8,128)(2,1)S(1)}, bf16[96,768]{1,0:T(8,128)(2,1)S(1)}, u32[]{:S(2)}, u32[]{:S(2)}) collective-permute-start(bf16[96,768]{1,0:T(8,128)(2,1)S(1)} %pad_maximum_fusion.13), channel_id=1, source_target_pairs={{0,4},{4,0},{8,12},{12,8},{16,20},{20,16},{24,28},{28,24},{1,5},{5... | collective-permute-start | bytes 442376 | tf_op jit(solution)/shard_map/ppermute | solution.py:209
  175.3 5.6 %collective-permute-start.9 = (bf16[48,576]{0,1:T(8,128)(2,1)S(1)}, bf16[48,576]{0,1:T(8,128)(2,1)S(1)}, u32[]{:S(2)}, u32[]{:S(2)}) collective-permute-start(bf16[48,576]{0,1:T(8,128)(2,1)S(1)} %add_convert_fusion.9), channel_id=1, source_target_pairs={{0,4},{4,0},{8,12},{12,8},{16,20},{20,16},{24,28},{28,24},{1,5},{5... | collective-permute-start | bytes 165896 | tf_op jit(solution)/shard_map/ppermute | solution.py:209
  179.4 11.6 %collective-permute-start.3 = (bf16[48,576]{0,1:T(8,128)(2,1)S(1)}, bf16[48,576]{0,1:T(8,128)(2,1)S(1)}, u32[]{:S(2)}, u32[]{:S(2)}) collective-permute-start(bf16[48,576]{0,1:T(8,128)(2,1)S(1)} %add_convert_fusion.11), channel_id=1, source_target_pairs={{0,16},{4,20},{8,24},{12,28},{16,0},{20,4},{24,8},{28,12},{1,17},{... | collective-permute-start | bytes 165896 | tf_op jit(solution)/shard_map/ppermute | solution.py:209
  181.0 11.6 %collective-permute-start.10 = (bf16[96,576]{0,1:T(8,128)(2,1)S(1)}, bf16[96,576]{0,1:T(8,128)(2,1)S(1)}, u32[]{:S(2)}, u32[]{:S(2)}) collective-permute-start(bf16[96,576]{0,1:T(8,128)(2,1)S(1)} %pad_maximum_fusion.12), channel_id=1, source_target_pairs={{0,16},{4,20},{8,24},{12,28},{16,0},{20,4},{24,8},{28,12},{1,17},{... | collective-permute-start | bytes 331784 | tf_op jit(solution)/shard_map/ppermute | solution.py:209
  191.1 6.8 %collective-permute-start.4 = (bf16[96,576]{0,1:T(8,128)(2,1)S(1)}, bf16[96,576]{0,1:T(8,128)(2,1)S(1)}, u32[]{:S(2)}, u32[]{:S(2)}) collective-permute-start(bf16[96,576]{0,1:T(8,128)(2,1)S(1)} %pad_maximum_fusion.11), channel_id=1, source_target_pairs={{0,8},{4,12},{8,0},{12,4},{16,24},{20,28},{24,16},{28,20},{1,9},{5... | collective-permute-start | bytes 331784 | tf_op jit(solution)/shard_map/ppermute | solution.py:209
  192.9 15.9 %collective-permute-start.11 = (bf16[192,576]{0,1:T(8,128)(2,1)S(1)}, bf16[192,576]{0,1:T(8,128)(2,1)S(1)}, u32[]{:S(2)}, u32[]{:S(2)}) collective-permute-start(bf16[192,576]{0,1:T(8,128)(2,1)S(1)} %pad_maximum_fusion.6), channel_id=1, source_target_pairs={{0,8},{4,12},{8,0},{12,4},{16,24},{20,28},{24,16},{28,20},{1,9},{5... | collective-permute-start | bytes 663560 | tf_op jit(solution)/shard_map/ppermute | solution.py:209
  198.3 46.4 %collective-permute-start.5 = (bf16[192,576]{0,1:T(8,128)(2,1)S(1)}, bf16[192,576]{0,1:T(8,128)(2,1)S(1)}, u32[]{:S(2)}, u32[]{:S(2)}) collective-permute-start(bf16[192,576]{0,1:T(8,128)(2,1)S(1)} %pad_maximum_fusion.5), channel_id=1, source_target_pairs={{0,4},{4,0},{8,12},{12,8},{16,20},{20,16},{24,28},{28,24},{1,5},{5... | collective-permute-start | bytes 663560 | tf_op jit(solution)/shard_map/ppermute | solution.py:209
  200.1 13.2 %collective-permute-start.28 = (bf16[192,768]{1,0:T(8,128)(2,1)S(1)}, bf16[192,768]{1,0:T(8,128)(2,1)S(1)}, u32[]{:S(2)}, u32[]{:S(2)}) collective-permute-start(bf16[192,768]{1,0:T(8,128)(2,1)S(1)} %broadcast_select_fusion.8), channel_id=1, source_target_pairs={{0,8},{4,12},{8,0},{12,4},{16,24},{20,28},{24,16},{28,20},{1,9},{5... | collective-permute-start | bytes 884744 | tf_op jit(solution)/shard_map/ppermute | solution.py:209
  201.5 17.3 %collective-permute-start.22 = (bf16[192,768]{1,0:T(8,128)(2,1)S(1)}, bf16[192,768]{1,0:T(8,128)(2,1)S(1)}, u32[]{:S(2)}, u32[]{:S(2)}) collective-permute-start(bf16[192,768]{1,0:T(8,128)(2,1)S(1)} %broadcast_select_fusion.11), channel_id=1, source_target_pairs={{0,16},{4,20},{8,24},{12,28},{16,0},{20,4},{24,8},{28,12},{1,17},{... | collective-permute-start | bytes 884744 | tf_op jit(solution)/shard_map/ppermute | solution.py:209
  213.5 7.8 %collective-permute-start.29 = (bf16[96,768]{1,0:T(8,128)(2,1)S(1)}, bf16[96,768]{1,0:T(8,128)(2,1)S(1)}, u32[]{:S(2)}, u32[]{:S(2)}) collective-permute-start(bf16[96,768]{1,0:T(8,128)(2,1)S(1)} %broadcast_select_fusion.22), channel_id=1, source_target_pairs={{0,16},{4,20},{8,24},{12,28},{16,0},{20,4},{24,8},{28,12},{1,17},{... | collective-permute-start | bytes 442376 | tf_op jit(solution)/shard_map/ppermute | solution.py:209
  219.0 5.9 %collective-permute-start.23 = (bf16[96,768]{1,0:T(8,128)(2,1)S(1)}, bf16[96,768]{1,0:T(8,128)(2,1)S(1)}, u32[]{:S(2)}, u32[]{:S(2)}) collective-permute-start(bf16[96,768]{1,0:T(8,128)(2,1)S(1)} %broadcast_select_fusion.25), channel_id=1, source_target_pairs={{0,4},{4,0},{8,12},{12,8},{16,20},{20,16},{24,28},{28,24},{1,5},{5... | collective-permute-start | bytes 442376 | tf_op jit(solution)/shard_map/ppermute | solution.py:209
  221.3 8.8 %collective-permute-start.30 = (bf16[96,768]{1,0:T(8,128)(2,1)S(1)}, bf16[96,768]{1,0:T(8,128)(2,1)S(1)}, u32[]{:S(2)}, u32[]{:S(2)}) collective-permute-start(bf16[96,768]{1,0:T(8,128)(2,1)S(1)} %add_convert_fusion.6), channel_id=1, source_target_pairs={{0,16},{4,20},{8,24},{12,28},{16,0},{20,4},{24,8},{28,12},{1,17},{... | collective-permute-start | bytes 442376 | tf_op jit(solution)/shard_map/ppermute | solution.py:209
  224.9 5.3 %collective-permute-start.24 = (bf16[96,768]{1,0:T(8,128)(2,1)S(1)}, bf16[96,768]{1,0:T(8,128)(2,1)S(1)}, u32[]{:S(2)}, u32[]{:S(2)}) collective-permute-start(bf16[96,768]{1,0:T(8,128)(2,1)S(1)} %add_convert_fusion.7), channel_id=1, source_target_pairs={{0,4},{4,0},{8,12},{12,8},{16,20},{20,16},{24,28},{28,24},{1,5},{5... | collective-permute-start | bytes 442376 | tf_op jit(solution)/shard_map/ppermute | solution.py:209
  230.1 14.3 %collective-permute-start.31 = (bf16[192,768]{1,0:T(8,128)(2,1)S(1)}, bf16[192,768]{1,0:T(8,128)(2,1)S(1)}, u32[]{:S(2)}, u32[]{:S(2)}) collective-permute-start(bf16[192,768]{1,0:T(8,128)(2,1)S(1)} %pad_maximum_fusion.8), channel_id=1, source_target_pairs={{0,8},{4,12},{8,0},{12,4},{16,24},{20,28},{24,16},{28,20},{1,9},{5... | collective-permute-start | bytes 884744 | tf_op jit(solution)/shard_map/ppermute | solution.py:209
  230.3 16.3 %collective-permute-start.25 = (bf16[192,768]{1,0:T(8,128)(2,1)S(1)}, bf16[192,768]{1,0:T(8,128)(2,1)S(1)}, u32[]{:S(2)}, u32[]{:S(2)}) collective-permute-start(bf16[192,768]{1,0:T(8,128)(2,1)S(1)} %pad_maximum_fusion.7), channel_id=1, source_target_pairs={{0,16},{4,20},{8,24},{12,28},{16,0},{20,4},{24,8},{28,12},{1,17},{... | collective-permute-start | bytes 884744 | tf_op jit(solution)/shard_map/ppermute | solution.py:209
  244.6 14.5 %collective-permute-start.32 = (bf16[384,768]{1,0:T(8,128)(2,1)S(1)}, bf16[384,768]{1,0:T(8,128)(2,1)S(1)}, u32[]{:S(2)}, u32[]{:S(2)}) collective-permute-start(bf16[384,768]{1,0:T(8,128)(2,1)S(1)} %pad_maximum_fusion.4), channel_id=1, source_target_pairs={{0,4},{4,0},{8,12},{12,8},{16,20},{20,16},{24,28},{28,24},{1,5},{5... | collective-permute-start | bytes 1769480 | tf_op jit(solution)/shard_map/ppermute | solution.py:209
  246.7 14.5 %collective-permute-start.26 = (bf16[384,768]{1,0:T(8,128)(2,1)S(1)}, bf16[384,768]{1,0:T(8,128)(2,1)S(1)}, u32[]{:S(2)}, u32[]{:S(2)}) collective-permute-start(bf16[384,768]{1,0:T(8,128)(2,1)S(1)} %pad_maximum_fusion.3), channel_id=1, source_target_pairs={{0,8},{4,12},{8,0},{12,4},{16,24},{20,28},{24,16},{28,20},{1,9},{5... | collective-permute-start | bytes 1769480 | tf_op jit(solution)/shard_map/ppermute | solution.py:209
  (17 other events, 23.3 us)
